TPU v7x, 512 devices: a whole 4x8x8 slice. The times are simulated.
512 devices in a mesh: gx: 32 (over y, x), gy: 16 (over z, core).
Axes of the slice: x: 4, y: 8, z: 8, core: 2. Of those that a mesh axis runs over, the one named last changes fastest.
Arguments:
- tracer_now: float32 [2, 32, 256, 4096], P(None, None, 'gy', 'gx'), may hold values from -6 to 6
- velocity_now: float32 [2, 32, 256, 4096], P(None, None, 'gy', 'gx'), may hold values from -6 to 6
- tracer_old: float32 [2, 32, 256, 4096], P(None, None, 'gy', 'gx'), may hold values from -6 to 6
- velocity_old: float32 [2, 32, 256, 4096], P(None, None, 'gy', 'gx'), may hold values from -6 to 6
- depth_levels: int32 [256, 4096], P('gy', 'gx'), may hold values from 0 to 32
- land_blocks: int32 [32, 512], P('gy', 'gx'), may hold values 0 or 1
Outputs:
- tracer_next: float32 [2, 32, 256, 4096], P(None, None, 'gy', 'gx')
- velocity_next: float32 [2, 32, 256, 4096], P(None, None, 'gy', 'gx')
- surface_height: float32 [256, 4096], P('gy', 'gx')
- residual: float32 [256, 4096], P('gy', 'gx')
Inputs may be any that keep to these rules, and one draw needn't show every extreme that they name: `depth_levels`: 0 marks a land column.
All inputs are finite; a program needn't handle non-finite values. No bound on the sum of `land_blocks` on one device may be relied on, other than what follows from the above.
Results may differ from a plain program's by a relative error of at most 0.0003.
Values sent between devices are 32-bit elements; how exact they have to be, the bound alone decides.
No kernel may reach another device: no remote copies, remote signals or barrier semaphores. Data moves between devices by JAX's collectives and lax.ppermute only.
A program may use at most 64 MiB of HBM per device.

v0:
```python
import jax
import jax.numpy as jnp
from jax import lax
from jax.sharding import PartitionSpec as P

BLOCK = 8
ITERS = 4


STEP_TWICE = 0.1
TRACER_MIX = 0.05
MOMENTUM_MIX = 0.05
HEAT_EXPANSION = 0.2
SALT_CONTRACTION = 0.15
PRESSURE_SCALE = 0.2
SURFACE_TERM = 1.0
SIDES = ((0, 1), (0, -1), (1, 0), (-1, 0))
ALL_SIDES = (
    (0, 1, 1.0),
    (0, -1, 1.0),
    (1, 0, 1.0),
    (-1, 0, 1.0),
    (1, 1, 0.5),
    (1, -1, 0.5),
    (-1, 1, 0.5),
    (-1, -1, 0.5),
)


def padded_2(block, sides, width):
    for axis, dim in sides:
        count = lax.axis_size(axis)
        forward = [(i, i + 1) for i in range(count - 1)]
        forward.append((count - 1, 0))
        backward = [(target, source) for source, target in forward]
        low = lax.ppermute(
            lax.slice_in_dim(block, block.shape[dim] - width, None, axis=dim), axis, forward
        )
        high = lax.ppermute(lax.slice_in_dim(block, 0, width, axis=dim), axis, backward)
        block = jnp.concatenate([low, block, high], axis=dim)
    return block


def offset(array, row_step, col_step):
    rows = array.shape[-2] - 2
    cols = array.shape[-1] - 2
    return array[..., 1 + row_step : 1 + row_step + rows, 1 + col_step : 1 + col_step + cols]


def interior(array):
    return offset(array, 0, 0)


def laplace(field, mask):
    center = interior(field)
    mask_mid = interior(mask)
    result = jnp.zeros_like(center)
    for row_step, col_step in SIDES:
        result = result + mask_mid * offset(mask, row_step, col_step) * (
            offset(field, row_step, col_step) - center
        )
    return result


def biharmonic(field, mask):
    first = interior(mask) * laplace(field, mask)
    return laplace(first, interior(mask))


def advect(tracer, eastward, northward, mask):
    center = interior(tracer)
    mask_mid = interior(mask)
    result = jnp.zeros_like(center)
    for row_step, col_step in SIDES:
        speed = northward if row_step != 0 else eastward
        orient = float(row_step + col_step)
        face = (
            mask_mid
            * offset(mask, row_step, col_step)
            * 0.5
            * (interior(speed) + offset(speed, row_step, col_step))
        )
        result = result + orient * face * 0.5 * (center + offset(tracer, row_step, col_step))
    return result


def gradient(pressure, mask, row_step, col_step):
    center = interior(pressure)
    mask_mid = interior(mask)
    ahead = (
        mask_mid
        * offset(mask, row_step, col_step)
        * (offset(pressure, row_step, col_step) - center)
    )
    behind = (
        mask_mid
        * offset(mask, -row_step, -col_step)
        * (center - offset(pressure, -row_step, -col_step))
    )
    return 0.5 * (ahead + behind)


def pressure_field(fields):
    density = (-HEAT_EXPANSION * fields[0] + SALT_CONTRACTION * fields[1]) * fields[8]
    return PRESSURE_SCALE * jnp.cumsum(density, axis=0)


def coriolis_rows(first_row, count, rows_global):
    rows = (first_row + jnp.arange(count, dtype=jnp.int32)).astype(jnp.float32)
    return (2.0 * (rows + 0.5) / rows_global - 1.0)[:, None]


def evolve(fields, pressure, coriolis):
    mask_two = fields[8]
    mask_one = interior(mask_two)
    mask_zero = interior(mask_one)
    temp_now = interior(fields[0])
    salt_now = interior(fields[1])
    east_now = interior(fields[2])
    north_now = interior(fields[3])
    press_one = interior(pressure)
    cor_zero = coriolis[2:-2]
    temp_next = mask_zero * (
        interior(interior(fields[4]))
        + STEP_TWICE
        * (
            -advect(temp_now, east_now, north_now, mask_one)
            - TRACER_MIX * biharmonic(fields[4], mask_two)
        )
    )
    salt_next = mask_zero * (
        interior(interior(fields[5]))
        + STEP_TWICE
        * (
            -advect(salt_now, east_now, north_now, mask_one)
            - TRACER_MIX * biharmonic(fields[5], mask_two)
        )
    )
    east_next = mask_zero * (
        interior(interior(fields[6]))
        + STEP_TWICE
        * (
            cor_zero * interior(north_now)
            - gradient(press_one, mask_one, 0, 1)
            - MOMENTUM_MIX * biharmonic(fields[6], mask_two)
        )
    )
    north_next = mask_zero * (
        interior(interior(fields[7]))
        + STEP_TWICE
        * (
            -cor_zero * interior(east_now)
            - gradient(press_one, mask_one, 1, 0)
            - MOMENTUM_MIX * biharmonic(fields[7], mask_two)
        )
    )
    return jnp.stack([temp_next, salt_next, east_next, north_next], 0)


def divergence_source(transports, top_band):
    east_part = 0.5 * (offset(transports[0], 0, 1) - offset(transports[0], 0, -1))
    north_part = 0.5 * (offset(transports[1], 1, 0) - offset(transports[1], -1, 0))
    return -interior(top_band) * (east_part + north_part)


def couplings(depth_band, top_band):
    weights = []
    diagonal = jnp.full(interior(depth_band).shape, SURFACE_TERM, jnp.float32)
    for row_step, col_step, factor in ALL_SIDES:
        weight = (
            factor
            * 0.5
            * (interior(depth_band) + offset(depth_band, row_step, col_step))
            * interior(top_band)
            * offset(top_band, row_step, col_step)
        )
        weights.append(weight)
        diagonal = diagonal + weight
    return (weights, diagonal)


def apply_operator(padded, weights, diagonal):
    result = diagonal * interior(padded)
    for number, (row_step, col_step, factor) in enumerate(ALL_SIDES):
        result = result - weights[number] * offset(padded, row_step, col_step)
    return result


def clip_poles(array, margin, lat_rows):
    global_rows = (
        lax.axis_index("gy") * lat_rows - margin + jnp.arange(array.shape[-2], dtype=jnp.int32)
    )
    keep = (global_rows >= 0) & (global_rows < lat_rows * lax.axis_size("gy"))
    return array * keep.astype(array.dtype)[:, None]


def on_device(tracer_now, velocity_now, tracer_old, velocity_old, depth_levels, land_blocks):
    levels = tracer_now.shape[1]
    lat_rows = tracer_now.shape[2]
    open_cells = jnp.repeat(jnp.repeat(land_blocks, BLOCK, 0), BLOCK, 1)
    level_index = jnp.arange(levels, dtype=jnp.int32)[:, None, None]
    margin = 2
    wet_cells = (level_index < depth_levels[None]).astype(jnp.float32) * open_cells.astype(
        jnp.float32
    )[None]
    fields = jnp.concatenate(
        [tracer_now, velocity_now, tracer_old, velocity_old, wet_cells[None]], 0
    )
    padded = padded_2(fields, (("gx", 3), ("gy", 2)), margin)
    padded = clip_poles(padded, margin, lat_rows)
    first_row = lax.axis_index("gy") * lat_rows - margin
    coriolis = coriolis_rows(first_row, padded.shape[-2], lat_rows * lax.axis_size("gy"))
    pressure = pressure_field(padded)
    updated = evolve(padded, pressure, coriolis)
    band_lo = margin - 1
    band = padded[8, :, band_lo : padded.shape[-2] - band_lo, band_lo : padded.shape[-1] - band_lo]
    depth_band = jnp.sum(band, 0) / levels
    top_band = band[0]
    summed = jnp.sum(updated[2:4], 1) / levels
    transports = padded_2(summed, (("gx", 2), ("gy", 1)), 1)
    transports = clip_poles(transports, 1, lat_rows)
    source = divergence_source(transports, top_band)
    weights, diagonal = couplings(depth_band, top_band)
    residual = source
    solution = jnp.zeros_like(source)
    direction = jnp.zeros_like(source)
    image_dir = jnp.zeros_like(source)
    descent_old = jnp.float32(1.0)
    step_old = jnp.float32(1.0)
    for iteration in range(ITERS):
        search = residual / diagonal
        search_pad = padded_2(search, (("gx", 1), ("gy", 0)), 1)
        search_pad = clip_poles(search_pad, 1, lat_rows)
        image = apply_operator(search_pad, weights, diagonal)
        descent, curvature = lax.psum(
            (jnp.sum(residual * search), jnp.sum(image * search)), ("gx", "gy")
        )
        if iteration == 0:
            blend = jnp.float32(0.0)
            step_length = descent / curvature
        else:
            blend = descent / descent_old
            step_length = descent / (curvature - blend * descent / step_old)
        direction = search + blend * direction
        image_dir = image + blend * image_dir
        solution = solution + step_length * direction
        residual = residual - step_length * image_dir
        descent_old = descent
        step_old = step_length
    return (updated[0:2], updated[2:4], solution, residual)


def solution(mesh):
    in_specs = (
        P(None, None, "gy", "gx"),
        P(None, None, "gy", "gx"),
        P(None, None, "gy", "gx"),
        P(None, None, "gy", "gx"),
        P("gy", "gx"),
        P("gy", "gx"),
    )
    out_specs = (P(None, None, "gy", "gx"), P(None, None, "gy", "gx"), P("gy", "gx"), P("gy", "gx"))
    return jax.shard_map(
        on_device, mesh=mesh, in_specs=in_specs, out_specs=out_specs, check_vma=False
    )
```

profile of v0, /device:TPU:1, one launch (start us, length us, event | category | flops | bytes accessed | tf_op | source)
XLA Modules:
  0.0 562.1 jit_solution(6319802707752151139)
XLA Ops:
  0.7 0.8 convert_element_type.41
  1.6 1.1 constant_dynamic-update-slice_fusion.3
  2.7 1.1 constant_dynamic-update-slice_fusion.2
  3.9 2.9 fusion.190
  6.8 2.6 copy.17
  9.5 8.1 %collective-permute-start.1 = (f32[9,32,16,2]{1,2,3,0:T(8,128)S(1)}, f32[9,32,16,2]{1,2,3,0:T(8,128)S(1)}, u32[]{:S(2)}, u32[]{:S(2)}) collective-permute-start(f32[9,32,16,2]{1,2,3,0:T(8,128)S(1)} %copy.17), channel_id=1, source_target_pairs={{16,0},{32,16},{48,32},{64,48},{80,64},{96,80},{112,96},{128,112},... | collective-permute-start | bytes 110600 | tf_op jit(solution)/shard_map/ppermute | solution.py:39
  17.6 2.6 copy.16
  20.2 2.1 collective-permute-start
  22.4 7.5 %collective-permute-done = f32[9,32,16,2]{1,2,3,0:T(8,128)S(1)} collective-permute-done((f32[9,32,16,2]{1,2,3,0:T(8,128)S(1)}, f32[9,32,16,2]{1,2,3,0:T(8,128)S(1)}, u32[]{:S(2)}, u32[]{:S(2)}) %collective-permute-start) | collective-permute-done | bytes 36896 | tf_op jit(solution)/shard_map/ppermute | solution.py:36
  29.8 2.4 copy.18
  32.2 2.4 copy.19
  34.6 4.4 pad_maximum_fusion.2
  38.9 3.9 collective-permute-start.2
  42.9 6.7 %collective-permute-done.2 = f32[9,32,2,132]{3,2,1,0:T(2,128)S(1)} collective-permute-done((f32[9,32,2,132]{3,2,1,0:T(2,128)S(1)}, f32[9,32,2,132]{3,2,1,0:T(2,128)S(1)}, u32[]{:S(2)}, u32[]{:S(2)}) %collective-permute-start.2) | collective-permute-done | bytes 304160 | tf_op jit(solution)/shard_map/ppermute | solution.py:36
  49.6 2.8 collective-permute-done.3
  52.4 3.8 maximum_multiply_fusion
  56.5 1.5 slice_bitcast_fusion
  58.0 1.7 fusion.2
  59.7 1.7 fusion.10
  61.4 1.0 fusion.66
  62.5 0.9 fusion.48
  63.4 0.8 fusion.189
  64.3 1.9 collective-permute-start.4
  66.2 6.9 %collective-permute-start.5 = (f32[2,16,1]{2,1,0:T(8,128)S(1)}, f32[2,16,1]{2,1,0:T(8,128)S(1)}, u32[]{:S(2)}, u32[]{:S(2)}) collective-permute-start(f32[2,16,1]{2,1,0:T(8,128)S(1)} %get-tuple-element.72), channel_id=1, source_target_pairs={{16,0},{32,16},{48,32},{64,48},{80,64},{96,80},{112,96},{128,112},... | collective-permute-start | bytes 392 | tf_op jit(solution)/shard_map/ppermute | solution.py:39
  73.2 1.7 fusion.18
  75.5 3.6 collective-permute-start.7
  80.2 1.9 collective-permute-start.8
  82.2 6.7 %collective-permute-start.9 = (f32[16,1]{1,0:T(8,128)S(1)}, f32[16,1]{1,0:T(8,128)S(1)}, u32[]{:S(2)}, u32[]{:S(2)}) collective-permute-start(f32[16,1]{1,0:T(8,128)S(1)} %get-tuple-element.80), channel_id=1, source_target_pairs={{16,0},{32,16},{48,32},{64,48},{80,64},{96,80},{112,96},{128,112},... | collective-permute-start | bytes 200 | tf_op jit(solution)/shard_map/ppermute | solution.py:39
  88.9 0.8 collective-permute-done.9
  89.7 4.6 collective-permute-start.11
  94.3 2.1 fusion.84
  97.1 101.3 %all-reduce.3 = (f32[]{:T(128)}, f32[]{:T(128)}) all-reduce(f32[]{:T(128)} %get-tuple-element.11, f32[]{:T(128)} %get-tuple-element.10), channel_id=1, replica_groups=mesh['gx'=32,'gy'=16] {'gx','gy'}, use_global_device_ids=true, to_apply=%region_4.5 | all-reduce | flops 2 | bytes 16 | tf_op jit(solution)/shard_map/psum | solution.py:235
  199.9 1.9 collective-permute-start.12
  201.8 6.7 %collective-permute-start.13 = (f32[16,1]{1,0:T(8,128)S(1)}, f32[16,1]{1,0:T(8,128)S(1)}, u32[]{:S(2)}, u32[]{:S(2)}) collective-permute-start(f32[16,1]{1,0:T(8,128)S(1)} %get-tuple-element.78), channel_id=1, source_target_pairs={{16,0},{32,16},{48,32},{64,48},{80,64},{96,80},{112,96},{128,112},... | collective-permute-start | bytes 200 | tf_op jit(solution)/shard_map/ppermute | solution.py:39
  209.3 1.6 collective-permute-start.14
  211.2 2.6 fusion.26
  214.7 100.6 %all-reduce.2 = (f32[]{:T(128)}, f32[]{:T(128)}) all-reduce(f32[]{:T(128)} %get-tuple-element.9, f32[]{:T(128)} %get-tuple-element.8), channel_id=1, replica_groups=mesh['gx'=32,'gy'=16] {'gx','gy'}, use_global_device_ids=true, to_apply=%region_8.9 | all-reduce | flops 2 | bytes 16 | tf_op jit(solution)/shard_map/psum | solution.py:235
  319.7 1.9 collective-permute-start.16
  321.6 6.7 %collective-permute-start.17 = (f32[16,1]{1,0:T(8,128)S(1)}, f32[16,1]{1,0:T(8,128)S(1)}, u32[]{:S(2)}, u32[]{:S(2)}) collective-permute-start(f32[16,1]{1,0:T(8,128)S(1)} %get-tuple-element.76), channel_id=1, source_target_pairs={{16,0},{32,16},{48,32},{64,48},{80,64},{96,80},{112,96},{128,112},... | collective-permute-start | bytes 200 | tf_op jit(solution)/shard_map/ppermute | solution.py:39
  329.2 1.7 collective-permute-start.18
  331.1 6.0 %fusion.105 = f32[1,32,16,128]{3,2,1,0:T(8,128)} fusion(f32[32,16,128]{2,1,0:T(8,128)} %copy-done.2, f32[32,18,130]{2,1,0:T(8,128)} %fusion.26, f32[32,16,128]{2,1,0:T(8,128)S(1)} %get-tuple-element.44, f32[32,20,132]{2,1,0:T(8,128)} %get-tuple-element.51, f32[32,20,132]{2,1,0:T(8,128)S(1)} %get-tuple-element.53, f32[32,20,132]{2,1,0:T(8,128)S(1)} %get-tuple-element.52, ...), kind=kLoop, calls=%fused_computation.161 | loop fusion | flops 3014656 | bytes 6029312 | tf_op jit(solution)/shard_map/stack | solution.py:157
  337.9 99.4 %all-reduce.1 = (f32[]{:T(128)}, f32[]{:T(128)}) all-reduce(f32[]{:T(128)} %get-tuple-element.7, f32[]{:T(128)} %get-tuple-element.6), channel_id=1, replica_groups=mesh['gx'=32,'gy'=16] {'gx','gy'}, use_global_device_ids=true, to_apply=%region_12.13 | all-reduce | flops 2 | bytes 16 | tf_op jit(solution)/shard_map/psum | solution.py:235
  441.2 1.9 collective-permute-start.20
  443.1 6.7 %collective-permute-start.21 = (f32[16,1]{1,0:T(8,128)S(1)}, f32[16,1]{1,0:T(8,128)S(1)}, u32[]{:S(2)}, u32[]{:S(2)}) collective-permute-start(f32[16,1]{1,0:T(8,128)S(1)} %get-tuple-element.74), channel_id=1, source_target_pairs={{16,0},{32,16},{48,32},{64,48},{80,64},{96,80},{112,96},{128,112},... | collective-permute-start | bytes 200 | tf_op jit(solution)/shard_map/ppermute | solution.py:39
  449.8 0.8 collective-permute-done.21
  450.7 1.3 collective-permute-start.22
  452.5 1.9 pad_maximum_fusion.3
  455.8 101.7 %all-reduce = (f32[]{:T(128)}, f32[]{:T(128)}) all-reduce(f32[]{:T(128)} %get-tuple-element.5, f32[]{:T(128)} %get-tuple-element.4), channel_id=1, replica_groups=mesh['gx'=32,'gy'=16] {'gx','gy'}, use_global_device_ids=true, to_apply=%region_16.17 | all-reduce | flops 2 | bytes 16 | tf_op jit(solution)/shard_map/psum | solution.py:235
  (78 shorter events, 10.2 us)
Async XLA Ops:
  0.6 3.1 copy-start.3
  0.6 3.2 copy-start.4
  0.7 3.2 copy-start.5
  9.5 22.7 %collective-permute-start.1 = (f32[9,32,16,2]{1,2,3,0:T(8,128)S(1)}, f32[9,32,16,2]{1,2,3,0:T(8,128)S(1)}, u32[]{:S(2)}, u32[]{:S(2)}) collective-permute-start(f32[9,32,16,2]{1,2,3,0:T(8,128)S(1)} %copy.17), channel_id=1, source_target_pairs={{16,0},{32,16},{48,32},{64,48},{80,64},{96,80},{112,96},{128,112},... | collective-permute-start | bytes 110600 | tf_op jit(solution)/shard_map/ppermute | solution.py:39
  20.2 9.6 %collective-permute-start = (f32[9,32,16,2]{1,2,3,0:T(8,128)S(1)}, f32[9,32,16,2]{1,2,3,0:T(8,128)S(1)}, u32[]{:S(2)}, u32[]{:S(2)}) collective-permute-start(f32[9,32,16,2]{1,2,3,0:T(8,128)S(1)} %copy.16), channel_id=1, source_target_pairs={{0,16},{16,32},{32,48},{48,64},{64,80},{80,96},{96,112},{112,128},... | collective-permute-start | bytes 110600 | tf_op jit(solution)/shard_map/ppermute | solution.py:36
  34.6 17.8 %copy-start = (f32[9,32,16,2]{3,2,1,0:T(8,128)S(1)}, f32[9,32,16,2]{3,2,1,0:T(8,128)}, u32[]{:S(2)}) copy-start(f32[9,32,16,2]{3,2,1,0:T(8,128)} %copy.18) | copy-start | bytes 110596
  34.6 17.8 %copy-start.1 = (f32[9,32,16,2]{3,2,1,0:T(8,128)S(1)}, f32[9,32,16,2]{3,2,1,0:T(8,128)}, u32[]{:S(2)}) copy-start(f32[9,32,16,2]{3,2,1,0:T(8,128)} %copy.19) | copy-start | bytes 110596
  38.9 10.7 %collective-permute-start.2 = (f32[9,32,2,132]{3,2,1,0:T(2,128)S(1)}, f32[9,32,2,132]{3,2,1,0:T(2,128)S(1)}, u32[]{:S(2)}, u32[]{:S(2)}) collective-permute-start(f32[9,32,2,132]{3,2,1,0:T(2,128)S(1)} %get-tuple-element.55), channel_id=1, source_target_pairs={{0,1},{1,2},{2,3},{3,4},{4,5},{5,6},{6,7},{7,8},{8,9},{9,10},{10,1... | collective-permute-start | bytes 912392 | tf_op jit(solution)/shard_map/ppermute | solution.py:36
  42.8 9.6 %collective-permute-start.3 = (f32[9,32,2,132]{3,2,1,0:T(2,128)S(1)}, f32[9,32,2,132]{3,2,1,0:T(2,128)S(1)}, u32[]{:S(2)}, u32[]{:S(2)}) collective-permute-start(f32[9,32,2,132]{3,2,1,0:T(2,128)S(1)} %get-tuple-element.56), channel_id=1, source_target_pairs={{1,0},{2,1},{3,2},{4,3},{5,4},{6,5},{7,6},{8,7},{9,8},{10,9},{11,1... | collective-permute-start | bytes 912392 | tf_op jit(solution)/shard_map/ppermute | solution.py:39
  62.5 31.8 %copy-start.2 = (f32[32,16,128]{2,1,0:T(8,128)}, f32[32,16,128]{2,1,0:T(8,128)S(1)}, u32[]{:S(2)}) copy-start(f32[32,16,128]{2,1,0:T(8,128)S(1)} %get-tuple-element.45) | copy-start | bytes 786436
  64.3 10.8 %collective-permute-start.4 = (f32[2,16,1]{2,1,0:T(8,128)S(1)}, f32[2,16,1]{2,1,0:T(8,128)S(1)}, u32[]{:S(2)}, u32[]{:S(2)}) collective-permute-start(f32[2,16,1]{2,1,0:T(8,128)S(1)} %get-tuple-element.71), channel_id=1, source_target_pairs={{0,16},{16,32},{32,48},{48,64},{64,80},{80,96},{96,112},{112,128},... | collective-permute-start | bytes 392 | tf_op jit(solution)/shard_map/ppermute | solution.py:36
  66.2 8.9 %collective-permute-start.5 = (f32[2,16,1]{2,1,0:T(8,128)S(1)}, f32[2,16,1]{2,1,0:T(8,128)S(1)}, u32[]{:S(2)}, u32[]{:S(2)}) collective-permute-start(f32[2,16,1]{2,1,0:T(8,128)S(1)} %get-tuple-element.72), channel_id=1, source_target_pairs={{16,0},{32,16},{48,32},{64,48},{80,64},{96,80},{112,96},{128,112},... | collective-permute-start | bytes 392 | tf_op jit(solution)/shard_map/ppermute | solution.py:39
  75.2 4.5 collective-permute-start.6
  75.5 4.4 collective-permute-start.7
  80.2 8.6 %collective-permute-start.8 = (f32[16,1]{1,0:T(8,128)S(1)}, f32[16,1]{1,0:T(8,128)S(1)}, u32[]{:S(2)}, u32[]{:S(2)}) collective-permute-start(f32[16,1]{1,0:T(8,128)S(1)} %get-tuple-element.79), channel_id=1, source_target_pairs={{0,16},{16,32},{32,48},{48,64},{64,80},{80,96},{96,112},{112,128},... | collective-permute-start | bytes 200 | tf_op jit(solution)/shard_map/ppermute | solution.py:36
  82.2 7.5 %collective-permute-start.9 = (f32[16,1]{1,0:T(8,128)S(1)}, f32[16,1]{1,0:T(8,128)S(1)}, u32[]{:S(2)}, u32[]{:S(2)}) collective-permute-start(f32[16,1]{1,0:T(8,128)S(1)} %get-tuple-element.80), channel_id=1, source_target_pairs={{16,0},{32,16},{48,32},{64,48},{80,64},{96,80},{112,96},{128,112},... | collective-permute-start | bytes 200 | tf_op jit(solution)/shard_map/ppermute | solution.py:39
  89.7 6.6 %collective-permute-start.10 = (f32[1,130]{1,0:T(1,128)S(1)}, f32[1,130]{1,0:T(1,128)S(1)}, u32[]{:S(2)}, u32[]{:S(2)}) collective-permute-start(f32[1,130]{1,0:T(1,128)S(1)} %get-tuple-element.69), channel_id=1, source_target_pairs={{0,1},{1,2},{2,3},{3,4},{4,5},{5,6},{6,7},{7,8},{8,9},{9,10},{10,1... | collective-permute-start | bytes 1568 | tf_op jit(solution)/shard_map/ppermute | solution.py:36
  89.7 6.6 %collective-permute-start.11 = (f32[1,130]{1,0:T(1,128)S(1)}, f32[1,130]{1,0:T(1,128)S(1)}, u32[]{:S(2)}, u32[]{:S(2)}) collective-permute-start(f32[1,130]{1,0:T(1,128)S(1)} %get-tuple-element.70), channel_id=1, source_target_pairs={{1,0},{2,1},{3,2},{4,3},{5,4},{6,5},{7,6},{8,7},{9,8},{10,9},{11,1... | collective-permute-start | bytes 1568 | tf_op jit(solution)/shard_map/ppermute | solution.py:39
  199.9 8.6 %collective-permute-start.12 = (f32[16,1]{1,0:T(8,128)S(1)}, f32[16,1]{1,0:T(8,128)S(1)}, u32[]{:S(2)}, u32[]{:S(2)}) collective-permute-start(f32[16,1]{1,0:T(8,128)S(1)} %get-tuple-element.77), channel_id=1, source_target_pairs={{0,16},{16,32},{32,48},{48,64},{64,80},{80,96},{96,112},{112,128},... | collective-permute-start | bytes 200 | tf_op jit(solution)/shard_map/ppermute | solution.py:36
  201.8 7.5 %collective-permute-start.13 = (f32[16,1]{1,0:T(8,128)S(1)}, f32[16,1]{1,0:T(8,128)S(1)}, u32[]{:S(2)}, u32[]{:S(2)}) collective-permute-start(f32[16,1]{1,0:T(8,128)S(1)} %get-tuple-element.78), channel_id=1, source_target_pairs={{16,0},{32,16},{48,32},{64,48},{80,64},{96,80},{112,96},{128,112},... | collective-permute-start | bytes 200 | tf_op jit(solution)/shard_map/ppermute | solution.py:39
  209.3 4.5 collective-permute-start.14
  210.9 3.0 collective-permute-start.15
  319.7 8.6 %collective-permute-start.16 = (f32[16,1]{1,0:T(8,128)S(1)}, f32[16,1]{1,0:T(8,128)S(1)}, u32[]{:S(2)}, u32[]{:S(2)}) collective-permute-start(f32[16,1]{1,0:T(8,128)S(1)} %get-tuple-element.75), channel_id=1, source_target_pairs={{0,16},{16,32},{32,48},{48,64},{64,80},{80,96},{96,112},{112,128},... | collective-permute-start | bytes 200 | tf_op jit(solution)/shard_map/ppermute | solution.py:36
  321.6 7.5 %collective-permute-start.17 = (f32[16,1]{1,0:T(8,128)S(1)}, f32[16,1]{1,0:T(8,128)S(1)}, u32[]{:S(2)}, u32[]{:S(2)}) collective-permute-start(f32[16,1]{1,0:T(8,128)S(1)} %get-tuple-element.76), channel_id=1, source_target_pairs={{16,0},{32,16},{48,32},{64,48},{80,64},{96,80},{112,96},{128,112},... | collective-permute-start | bytes 200 | tf_op jit(solution)/shard_map/ppermute | solution.py:39
  329.2 7.9 %collective-permute-start.18 = (f32[1,130]{1,0:T(1,128)S(1)}, f32[1,130]{1,0:T(1,128)S(1)}, u32[]{:S(2)}, u32[]{:S(2)}) collective-permute-start(f32[1,130]{1,0:T(1,128)S(1)} %get-tuple-element.65), channel_id=1, source_target_pairs={{0,1},{1,2},{2,3},{3,4},{4,5},{5,6},{6,7},{7,8},{8,9},{9,10},{10,1... | collective-permute-start | bytes 1568 | tf_op jit(solution)/shard_map/ppermute | solution.py:36
  330.8 6.3 %collective-permute-start.19 = (f32[1,130]{1,0:T(1,128)S(1)}, f32[1,130]{1,0:T(1,128)S(1)}, u32[]{:S(2)}, u32[]{:S(2)}) collective-permute-start(f32[1,130]{1,0:T(1,128)S(1)} %get-tuple-element.66), channel_id=1, source_target_pairs={{1,0},{2,1},{3,2},{4,3},{5,4},{6,5},{7,6},{8,7},{9,8},{10,9},{11,1... | collective-permute-start | bytes 1568 | tf_op jit(solution)/shard_map/ppermute | solution.py:39
  441.2 8.6 %collective-permute-start.20 = (f32[16,1]{1,0:T(8,128)S(1)}, f32[16,1]{1,0:T(8,128)S(1)}, u32[]{:S(2)}, u32[]{:S(2)}) collective-permute-start(f32[16,1]{1,0:T(8,128)S(1)} %get-tuple-element.73), channel_id=1, source_target_pairs={{0,16},{16,32},{32,48},{48,64},{64,80},{80,96},{96,112},{112,128},... | collective-permute-start | bytes 200 | tf_op jit(solution)/shard_map/ppermute | solution.py:36
  443.1 7.5 %collective-permute-start.21 = (f32[16,1]{1,0:T(8,128)S(1)}, f32[16,1]{1,0:T(8,128)S(1)}, u32[]{:S(2)}, u32[]{:S(2)}) collective-permute-start(f32[16,1]{1,0:T(8,128)S(1)} %get-tuple-element.74), channel_id=1, source_target_pairs={{16,0},{32,16},{48,32},{64,48},{80,64},{96,80},{112,96},{128,112},... | collective-permute-start | bytes 200 | tf_op jit(solution)/shard_map/ppermute | solution.py:39
  450.7 3.7 collective-permute-start.22
  452.0 3.0 collective-permute-start.23
where the time goes:
time: 563 us; the launch traced here: 562 us
  blocking collectives  403 us (72%)
  starting transfers between devices  71.4 us (13%)
  other arithmetic  34.3 us (6%)
  waiting for transfers between devices  21.5 us (4%)
  local copies, waits for them, and re-layouts  17.3 us (3%)
  between operations  14.4 us (3%)
    psum x4, blocking collectives, on_device(): lax.psum((jnp.sum(residual * search), jnp.sum(image * search)), ('gx', 'g...  403 us
    ppermute x12, starting transfers between devices, padded_2(): lax.ppermute(lax.slice_in_dim(block, 0, width, axis=dim), axis, backward)  51.1 us
    ppermute x12, starting transfers between devices, padded_2(): lax.ppermute(lax.slice_in_dim(block, block.shape[dim] - width, None, axis...  20.3 us
    ppermute x12, waiting for transfers between devices, padded_2(): lax.ppermute(lax.slice_in_dim(block, block.shape[dim] - width, None, axis...  14.9 us
    another operation x5, other arithmetic, evolve(): return jnp.stack([temp_next, salt_next, east_next, north_next], 0)  11.8 us
  transfers between devices with their start and end apart: 24, of which 10 were waited for; matrix products, arithmetic and copies ran while one was open for 3% of the time, Pallas kernels for 0%

commit v1 on v0

--- a/solution.py
+++ b/solution.py
@@ -194,60 +194,140 @@
     return array * keep.astype(array.dtype)[:, None]
 
 
+def rim(block, width, rows, cols, lat_rows):
+    block = padded_2(block, (("gx", cols), ("gy", rows)), width)
+    return clip_poles(block, width, lat_rows)
+
+
+def neighbour_sum(padded, weights):
+    result = jnp.zeros_like(interior(padded))
+    for number, (row_step, col_step, factor) in enumerate(ALL_SIDES):
+        keep = weights[number]
+        result = result + keep * offset(padded, row_step, col_step)
+    return result
+
+
+def trim(array, width):
+    if width == 0:
+        return array
+    return array[..., width:-width, width:-width]
+
+
+CENTER = 0.2
+HALF = 0.6
+
+
+def basis(start, weights, diagonal):
+    inverse = 1.0 / diagonal
+    found = [start]
+    for step in range(ITERS):
+        last = found[-1]
+        kept = [trim(weight, step) for weight in weights]
+        image = neighbour_sum(last, kept) * trim(inverse, step)
+        image = (image - CENTER * interior(last)) * (1.0 / HALF)
+        if step > 0:
+            image = 2.0 * image - trim(found[-2], 2)
+        found.append(image)
+    return [trim(term, ITERS - number) for number, term in enumerate(found)]
+
+
+def total(values):
+    count = values.shape[0]
+    for axis in ("gy", "gx"):
+        size = lax.axis_size(axis)
+        spread = jnp.broadcast_to(values[None], (size, count))
+        values = jnp.sum(lax.all_to_all(spread, axis, 0, 0, tiled=True), 0)
+    return values
+
+
+def shifted_times(coefs):
+    out = [0.0] * (ITERS + 1)
+    for j in range(ITERS):
+        out[j] = out[j] + CENTER * coefs[j]
+        if j == 0:
+            out[1] = out[1] + HALF * coefs[0]
+        else:
+            out[j + 1] = out[j + 1] + 0.5 * HALF * coefs[j]
+            out[j - 1] = out[j - 1] + 0.5 * HALF * coefs[j]
+    return out
+
+
+def dot(left, gram, right):
+    result = 0.0
+    for i, a in enumerate(left):
+        for j, b in enumerate(right):
+            if isinstance(a, float) and a == 0.0 or isinstance(b, float) and b == 0.0:
+                continue
+            result = result + a * b * gram[min(i, j), max(i, j)]
+    return result
+
+
+def conjugate_gradients(gram):
+    size = ITERS + 1
+    z = [1.0] + [0.0] * ITERS
+    p = [0.0] * size
+    q = [0.0] * size
+    x = [0.0] * size
+    descent_old = step_old = None
+    for iteration in range(ITERS):
+        moved = shifted_times(z)
+        w = [a - b for a, b in zip(z, moved)]
+        descent = dot(z, gram, z)
+        curvature = dot(w, gram, z)
+        if iteration == 0:
+            step_length = descent / curvature
+            p, q = list(z), list(w)
+        else:
+            blend = descent / descent_old
+            step_length = descent / (curvature - blend * descent / step_old)
+            p = [a + blend * b for a, b in zip(z, p)]
+            q = [a + blend * b for a, b in zip(w, q)]
+        x = [a + step_length * b for a, b in zip(x, p)]
+        z = [a - step_length * b for a, b in zip(z, q)]
+        descent_old, step_old = descent, step_length
+    return x, z
+
+
 def on_device(tracer_now, velocity_now, tracer_old, velocity_old, depth_levels, land_blocks):
     levels = tracer_now.shape[1]
     lat_rows = tracer_now.shape[2]
     open_cells = jnp.repeat(jnp.repeat(land_blocks, BLOCK, 0), BLOCK, 1)
-    level_index = jnp.arange(levels, dtype=jnp.int32)[:, None, None]
+    wide = ITERS + 1
     margin = 2
-    wet_cells = (level_index < depth_levels[None]).astype(jnp.float32) * open_cells.astype(
-        jnp.float32
-    )[None]
-    fields = jnp.concatenate(
-        [tracer_now, velocity_now, tracer_old, velocity_old, wet_cells[None]], 0
-    )
-    padded = padded_2(fields, (("gx", 3), ("gy", 2)), margin)
-    padded = clip_poles(padded, margin, lat_rows)
+    depths = rim((depth_levels * open_cells).astype(jnp.float32), wide, 0, 1, lat_rows)
+    level_index = jnp.arange(levels, dtype=jnp.int32)[:, None, None].astype(jnp.float32)
+    wet = (level_index < trim(depths, wide - margin)[None]).astype(jnp.float32)
+    fields = jnp.concatenate([tracer_now, velocity_now, tracer_old, velocity_old], 0)
+    padded = rim(fields, margin, 2, 3, lat_rows)
+    padded = jnp.concatenate([padded, wet[None]], 0)
     first_row = lax.axis_index("gy") * lat_rows - margin
     coriolis = coriolis_rows(first_row, padded.shape[-2], lat_rows * lax.axis_size("gy"))
     pressure = pressure_field(padded)
     updated = evolve(padded, pressure, coriolis)
-    band_lo = margin - 1
-    band = padded[8, :, band_lo : padded.shape[-2] - band_lo, band_lo : padded.shape[-1] - band_lo]
-    depth_band = jnp.sum(band, 0) / levels
-    top_band = band[0]
+    depth_band = depths / levels
+    top_band = (depths > 0).astype(jnp.float32)
     summed = jnp.sum(updated[2:4], 1) / levels
-    transports = padded_2(summed, (("gx", 2), ("gy", 1)), 1)
-    transports = clip_poles(transports, 1, lat_rows)
+    transports = rim(summed, wide, 1, 2, lat_rows)
     source = divergence_source(transports, top_band)
     weights, diagonal = couplings(depth_band, top_band)
-    residual = source
-    solution = jnp.zeros_like(source)
-    direction = jnp.zeros_like(source)
-    image_dir = jnp.zeros_like(source)
-    descent_old = jnp.float32(1.0)
-    step_old = jnp.float32(1.0)
-    for iteration in range(ITERS):
-        search = residual / diagonal
-        search_pad = padded_2(search, (("gx", 1), ("gy", 0)), 1)
-        search_pad = clip_poles(search_pad, 1, lat_rows)
-        image = apply_operator(search_pad, weights, diagonal)
-        descent, curvature = lax.psum(
-            (jnp.sum(residual * search), jnp.sum(image * search)), ("gx", "gy")
-        )
-        if iteration == 0:
-            blend = jnp.float32(0.0)
-            step_length = descent / curvature
-        else:
-            blend = descent / descent_old
-            step_length = descent / (curvature - blend * descent / step_old)
-        direction = search + blend * direction
-        image_dir = image + blend * image_dir
-        solution = solution + step_length * direction
-        residual = residual - step_length * image_dir
-        descent_old = descent
-        step_old = step_length
-    return (updated[0:2], updated[2:4], solution, residual)
+    terms = basis(source / diagonal, [trim(weight, 1) for weight in weights], trim(diagonal, 1))
+    diagonal = trim(diagonal, ITERS)
+    sums = []
+    for i in range(ITERS + 1):
+        scaled = diagonal * terms[i]
+        for j in range(i, ITERS + 1):
+            sums.append(jnp.sum(scaled * terms[j]))
+    sums = total(jnp.stack(sums))
+    gram = {}
+    count = 0
+    for i in range(ITERS + 1):
+        for j in range(i, ITERS + 1):
+            gram[i, j] = sums[count]
+            count += 1
+    x, z = conjugate_gradients(gram)
+    height = sum(c * term for c, term in zip(x[:ITERS], terms))
+    residual = diagonal * sum(c * term for c, term in zip(z, terms))
+    return (updated[0:2], updated[2:4], height, residual)
 
 
 def solution(mesh):

time: 563 us -> 215 us (0.38)
  blocking collectives: 403 us -> 33.6 us
  between operations: 14.4 us -> 79.7 us
  starting transfers between devices: 71.4 us -> 39.9 us
  waiting for transfers between devices: 21.5 us -> 9.26 us
  other arithmetic: 34.3 us -> 24.3 us
  local copies, waits for them, and re-layouts: 17.3 us -> 26.9 us
    psum x4 -> x0, blocking collectives: 403 us -> none  [on_device(): lax.psum((jnp.sum(residual * search), jnp.sum(image * search)), ('gx', 'g...]
    all_to_all x0 -> x2, blocking collectives: none -> 33.6 us  [total(): values = jnp.sum(lax.all_to_all(spread, axis, 0, 0, tiled=True), 0)]
    ppermute x12 -> x6, starting transfers between devices: 51.1 us -> 23.1 us  [padded_2(): lax.ppermute(lax.slice_in_dim(block, 0, width, axis=dim), axis, backward)]
    another operation x0 -> x1, local copies, waits for them, and re-layouts: none -> 9.48 us  [on_device(): sums = total(jnp.stack(sums))]
    ppermute x12 -> x6, waiting for transfers between devices: 14.9 us -> 5.46 us  [padded_2(): lax.ppermute(lax.slice_in_dim(block, block.shape[dim] - width, None, axis...]
    another operation x5 -> x4, other arithmetic: 11.8 us -> 4.92 us  [evolve(): return jnp.stack([temp_next, salt_next, east_next, north_next], 0)]
    ppermute x12 -> x6, starting transfers between devices: 20.3 us -> 16.8 us  [padded_2(): lax.ppermute(lax.slice_in_dim(block, block.shape[dim] - width, None, axis...]
  transfers between devices with their start and end apart: 24 -> 12, of which waited for: 10 -> 6; matrix products, arithmetic and copies ran while one was open for 3% -> 9% of each run, Pallas kernels for 0% -> 0%
where the time goes in v1:
time: 215 us; the launch traced here: 214 us
  between operations  79.7 us (37%)
  starting transfers between devices  39.9 us (19%)
  blocking collectives  33.6 us (16%)
  local copies, waits for them, and re-layouts  26.9 us (13%)
  other arithmetic  24.3 us (11%)
  waiting for transfers between devices  9.26 us (4%)
    all_to_all x2, blocking collectives, total(): values = jnp.sum(lax.all_to_all(spread, axis, 0, 0, tiled=True), 0)  33.6 us
    ppermute x6, starting transfers between devices, padded_2(): lax.ppermute(lax.slice_in_dim(block, 0, width, axis=dim), axis, backward)  23.1 us
    ppermute x6, starting transfers between devices, padded_2(): lax.ppermute(lax.slice_in_dim(block, block.shape[dim] - width, None, axis...  16.8 us
    another operation x1, local copies, waits for them, and re-layouts, on_device(): sums = total(jnp.stack(sums))  9.48 us
    mul x4, other arithmetic, biharmonic(): first = interior(mask) * laplace(field, mask)  6.87 us
    ppermute x6, waiting for transfers between devices, padded_2(): lax.ppermute(lax.slice_in_dim(block, block.shape[dim] - width, None, axis...  5.46 us
    slice x6, local copies, waits for them, and re-layouts, padded_2(): lax.slice_in_dim(block, block.shape[dim] - width, None, axis=dim)  5.19 us
    another operation x4, other arithmetic, evolve(): return jnp.stack([temp_next, salt_next, east_next, north_next], 0)  4.92 us
  transfers between devices with their start and end apart: 12, of which 6 were waited for; matrix products, arithmetic and copies ran while one was open for 9% of the time, Pallas kernels for 0%

profile of v1, /device:TPU:1, one launch (start us, length us, event | category | flops | bytes accessed | tf_op | source)
XLA Modules:
  0.0 213.7 jit_solution(5778206273128734678)
XLA Ops:
  0.7 0.7 copy-done
  1.4 0.8 copy.54
  2.3 3.9 %collective-permute-start = (f32[16,5]{0,1:T(8,128)S(1)}, f32[16,5]{0,1:T(8,128)S(1)}, u32[]{:S(2)}, u32[]{:S(2)}) collective-permute-start(f32[16,5]{0,1:T(8,128)S(1)} %get-tuple-element.63), channel_id=1, source_target_pairs={{0,16},{16,32},{32,48},{48,64},{64,80},{80,96},{96,112},{112,128},... | collective-permute-start | bytes 968 | tf_op jit(solution)/shard_map/ppermute | solution.py:36
  6.2 6.1 %collective-permute-start.1 = (f32[16,5]{0,1:T(8,128)S(1)}, f32[16,5]{0,1:T(8,128)S(1)}, u32[]{:S(2)}, u32[]{:S(2)}) collective-permute-start(f32[16,5]{0,1:T(8,128)S(1)} %get-tuple-element.64), channel_id=1, source_target_pairs={{16,0},{32,16},{48,32},{64,48},{80,64},{96,80},{112,96},{128,112},... | collective-permute-start | bytes 968 | tf_op jit(solution)/shard_map/ppermute | solution.py:39
  12.3 1.1 constant_dynamic-update-slice_fusion.3
  13.4 1.1 constant_dynamic-update-slice_fusion.2
  14.6 2.6 %fusion.192 = (f32[8,32,16,2]{3,2,1,0:T(8,128)}, f32[8,32,16,2]{3,2,1,0:T(8,128)}) fusion(f32[8,32,16,128]{3,2,1,0:T(8,128)S(1)} %constant_dynamic-update-slice_fusion), kind=kLoop, calls=%fused_computation.365 | loop fusion | bytes 131072 | tf_op jit(solution)/shard_map/slice | solution.py:37
  17.2 2.5 %copy.59 = f32[8,32,16,2]{1,2,3,0:T(8,128)S(1)} copy(f32[8,32,16,2]{3,2,1,0:T(8,128)} %get-tuple-element.58) | data formatting | bytes 65536 | tf_op jit(solution)/shard_map/slice | solution.py:39
  19.7 3.4 %collective-permute-start.5 = (f32[8,32,16,2]{1,2,3,0:T(8,128)S(1)}, f32[8,32,16,2]{1,2,3,0:T(8,128)S(1)}, u32[]{:S(2)}, u32[]{:S(2)}) collective-permute-start(f32[8,32,16,2]{1,2,3,0:T(8,128)S(1)} %copy.59), channel_id=1, source_target_pairs={{16,0},{32,16},{48,32},{64,48},{80,64},{96,80},{112,96},{128,112},... | collective-permute-start | bytes 98312 | tf_op jit(solution)/shard_map/ppermute | solution.py:39
  23.0 2.5 %copy.58 = f32[8,32,16,2]{1,2,3,0:T(8,128)S(1)} copy(f32[8,32,16,2]{3,2,1,0:T(8,128)} %get-tuple-element.57) | data formatting | bytes 65536 | tf_op jit(solution)/shard_map/slice | solution.py:37
  25.5 1.9 collective-permute-start.4
  27.9 3.5 %collective-permute-start.2 = (f32[5,138]{1,0:T(8,128)S(1)}, f32[5,138]{1,0:T(8,128)S(1)}, u32[]{:S(2)}, u32[]{:S(2)}) collective-permute-start(f32[5,138]{1,0:T(8,128)S(1)} %get-tuple-element.71), channel_id=1, source_target_pairs={{0,1},{1,2},{2,3},{3,4},{4,5},{5,6},{6,7},{7,8},{8,9},{9,10},{10,1... | collective-permute-start | bytes 8288 | tf_op jit(solution)/shard_map/ppermute | solution.py:36
  31.4 3.1 %collective-permute-start.3 = (f32[5,138]{1,0:T(8,128)S(1)}, f32[5,138]{1,0:T(8,128)S(1)}, u32[]{:S(2)}, u32[]{:S(2)}) collective-permute-start(f32[5,138]{1,0:T(8,128)S(1)} %get-tuple-element.72), channel_id=1, source_target_pairs={{1,0},{2,1},{3,2},{4,3},{5,4},{6,5},{7,6},{8,7},{9,8},{10,9},{11,1... | collective-permute-start | bytes 8288 | tf_op jit(solution)/shard_map/ppermute | solution.py:39
  34.5 2.1 %copy.60 = f32[8,32,16,2]{3,2,1,0:T(8,128)} copy(f32[8,32,16,2]{1,2,3,0:T(8,128)S(1)} %collective-permute-done.4) | data formatting | bytes 65536 | tf_op jit(solution)/shard_map/ppermute | solution.py:36
  36.7 2.2 %copy.61 = f32[8,32,16,2]{3,2,1,0:T(8,128)} copy(f32[8,32,16,2]{1,2,3,0:T(8,128)S(1)} %collective-permute-done.5) | data formatting | bytes 65536 | tf_op jit(solution)/shard_map/ppermute | solution.py:39
  38.9 4.1 %pad_maximum_fusion.2 = (f32[8,32,2,132]{3,2,1,0:T(2,128)S(1)}, f32[8,32,2,132]{3,2,1,0:T(2,128)S(1)}) fusion(f32[8,32,16,2]{3,2,1,0:T(8,128)} %copy.61, f32[8,32,16,128]{3,2,1,0:T(8,128)S(1)} %constant_dynamic-update-slice_fusion, f32[8,32,16,2]{3,2,1,0:T(8,128)} %copy.60), kind=kLoop, calls=%fused_computation.69 | loop fusion | flops 270336 | bytes 2703360 | tf_op jit(solution)/shard_map/slice | solution.py:37
  43.0 4.7 %collective-permute-start.6 = (f32[8,32,2,132]{3,2,1,0:T(2,128)S(1)}, f32[8,32,2,132]{3,2,1,0:T(2,128)S(1)}, u32[]{:S(2)}, u32[]{:S(2)}) collective-permute-start(f32[8,32,2,132]{3,2,1,0:T(2,128)S(1)} %get-tuple-element.55), channel_id=1, source_target_pairs={{0,1},{1,2},{2,3},{3,4},{4,5},{5,6},{6,7},{7,8},{8,9},{9,10},{10,1... | collective-permute-start | bytes 811016 | tf_op jit(solution)/shard_map/ppermute | solution.py:36
  47.6 1.1 collective-permute-start.7
  49.0 4.7 %collective-permute-done.6 = f32[8,32,2,132]{3,2,1,0:T(2,128)S(1)} collective-permute-done((f32[8,32,2,132]{3,2,1,0:T(2,128)S(1)}, f32[8,32,2,132]{3,2,1,0:T(2,128)S(1)}, u32[]{:S(2)}, u32[]{:S(2)}) %collective-permute-start.6) | collective-permute-done | bytes 270368 | tf_op jit(solution)/shard_map/ppermute | solution.py:36
  53.8 2.8 %collective-permute-done.7 = f32[8,32,2,132]{3,2,1,0:T(2,128)S(1)} collective-permute-done((f32[8,32,2,132]{3,2,1,0:T(2,128)S(1)}, f32[8,32,2,132]{3,2,1,0:T(2,128)S(1)}, u32[]{:S(2)}, u32[]{:S(2)}) %collective-permute-start.7) | collective-permute-done | bytes 270368 | tf_op jit(solution)/shard_map/ppermute | solution.py:39
  56.6 3.5 %maximum_multiply_fusion = f32[8,32,20,132]{3,2,1,0:T(8,128)S(1)} fusion(f32[8,32,2,132]{3,2,1,0:T(2,128)S(1)} %collective-permute-done.7, f32[8,32,16,2]{3,2,1,0:T(8,128)S(1)} %copy-done.2, f32[8,32,16,128]{3,2,1,0:T(8,128)S(1)} %constant_dynamic-update-slice_fusion, f32[8,32,16,2]{3,2,1,0:T(8,128)S(1)} %copy-done.1, ...), kind=kLoop, calls=%fused_computation | loop fusion | flops 3379200 | bytes 5406800 | tf_op jit(solution)/shard_map/mul | solution.py:194
  60.1 0.2 broadcast_multiply_fusion
  60.3 0.6 slice_bitcast_fusion
  60.9 1.7 fusion.3
  62.6 1.7 fusion.11
  64.4 1.7 fusion.19
  66.1 1.7 fusion.27
  67.8 1.1 fusion.66
  68.9 0.9 fusion.48
  69.8 1.4 fusion.84
  71.2 1.6 fusion.105
  72.7 1.0 fusion.191
  73.9 1.9 collective-permute-start.8
  75.8 6.7 %collective-permute-start.9 = (f32[2,16,5]{2,1,0:T(8,128)S(1)}, f32[2,16,5]{2,1,0:T(8,128)S(1)}, u32[]{:S(2)}, u32[]{:S(2)}) collective-permute-start(f32[2,16,5]{2,1,0:T(8,128)S(1)} %get-tuple-element.70), channel_id=1, source_target_pairs={{16,0},{32,16},{48,32},{64,48},{80,64},{96,80},{112,96},{128,112},... | collective-permute-start | bytes 1928 | tf_op jit(solution)/shard_map/ppermute | solution.py:39
  82.5 0.8 collective-permute-done.9
  83.4 0.9 collective-permute-start.10
  84.3 2.8 %collective-permute-start.11 = (f32[2,5,138]{2,1,0:T(8,128)S(1)}, f32[2,5,138]{2,1,0:T(8,128)S(1)}, u32[]{:S(2)}, u32[]{:S(2)}) collective-permute-start(f32[2,5,138]{2,1,0:T(8,128)S(1)} %get-tuple-element.66), channel_id=1, source_target_pairs={{1,0},{2,1},{3,2},{4,3},{5,4},{6,5},{7,6},{8,7},{9,8},{10,9},{11,1... | collective-permute-start | bytes 16568 | tf_op jit(solution)/shard_map/ppermute | solution.py:39
  87.1 0.6 collective-permute-done.10
  87.7 0.2 collective-permute-done.11
  88.4 0.2 slice_subtract_fusion.37
  88.5 0.2 slice_subtract_fusion.36
  88.7 0.8 multiply_reduce_fusion
  89.6 0.7 multiply_reduce_fusion.8
  90.3 9.5 %stack.86 = f32[15]{0:T(128)S(1)} concatenate(f32[1]{0:T(128)} %bitcast.16, f32[1]{0:T(128)} %bitcast.17, f32[1]{0:T(128)} %bitcast.18, f32[1]{0:T(128)} %bitcast.19, f32[1]{0:T(128)} %bitcast.20, f32[1]{0:T(128)} %bitcast.21, f32[1]{0:T(128)} %bitcast.22, f32[1]{0:T(128)} %bitcast.23, f32[1]{0:T(128)} %bitcast.24, f32[1]{0:T(128)} %bitcast.25, f32[1]{0:T(128)} %bitcast.26, ...), dimensions={0} | concatenate | bytes 120 | tf_op jit(solution)/shard_map/stack | solution.py:320
  99.8 17.4 %all_to_all.12 = f32[16,1,15]{2,1,0:T(1,128)S(1)} all-to-all(f32[16,1,15]{2,1,0:T(1,128)S(1)} %broadcast_in_dim.13), channel_id=1, replica_groups=mesh['gx'=32,'gy'=16] {'gy'}, dimensions={0} | all-to-all | bytes 1920 | tf_op jit(solution)/shard_map/all_to_all | solution.py:239
  117.2 16.2 %all_to_all.13 = f32[32,1,15]{2,1,0:T(1,128)S(1)} all-to-all(f32[32,1,15]{2,1,0:T(1,128)S(1)} %broadcast_in_dim.14), channel_id=1, replica_groups=mesh['gx'=32,'gy'=16] {'gx'}, dimensions={0} | all-to-all | bytes 3840 | tf_op jit(solution)/shard_map/all_to_all | solution.py:239
  133.5 0.7 fusion.197
  213.0 0.7 add_multiply_fusion
  (48 shorter events, 1.6 us)
Async XLA Ops:
  0.6 0.7 copy-start
  0.6 13.8 %copy-start.3 = (f32[2,32,16,128]{3,2,1,0:T(8,128)S(1)}, f32[2,32,16,128]{3,2,1,0:T(8,128)}, u32[]{:S(2)}) copy-start(f32[2,32,16,128]{3,2,1,0:T(8,128)} %param.8) | copy-start | bytes 1572868
  1.3 13.2 %copy-start.4 = (f32[2,32,16,128]{3,2,1,0:T(8,128)S(1)}, f32[2,32,16,128]{3,2,1,0:T(8,128)}, u32[]{:S(2)}) copy-start(f32[2,32,16,128]{3,2,1,0:T(8,128)} %param.9) | copy-start | bytes 1572868
  2.3 25.4 %collective-permute-start = (f32[16,5]{0,1:T(8,128)S(1)}, f32[16,5]{0,1:T(8,128)S(1)}, u32[]{:S(2)}, u32[]{:S(2)}) collective-permute-start(f32[16,5]{0,1:T(8,128)S(1)} %get-tuple-element.63), channel_id=1, source_target_pairs={{0,16},{16,32},{32,48},{48,64},{64,80},{80,96},{96,112},{112,128},... | collective-permute-start | bytes 968 | tf_op jit(solution)/shard_map/ppermute | solution.py:36
  6.2 21.5 %collective-permute-start.1 = (f32[16,5]{0,1:T(8,128)S(1)}, f32[16,5]{0,1:T(8,128)S(1)}, u32[]{:S(2)}, u32[]{:S(2)}) collective-permute-start(f32[16,5]{0,1:T(8,128)S(1)} %get-tuple-element.64), channel_id=1, source_target_pairs={{16,0},{32,16},{48,32},{64,48},{80,64},{96,80},{112,96},{128,112},... | collective-permute-start | bytes 968 | tf_op jit(solution)/shard_map/ppermute | solution.py:39
  19.7 17.0 %collective-permute-start.5 = (f32[8,32,16,2]{1,2,3,0:T(8,128)S(1)}, f32[8,32,16,2]{1,2,3,0:T(8,128)S(1)}, u32[]{:S(2)}, u32[]{:S(2)}) collective-permute-start(f32[8,32,16,2]{1,2,3,0:T(8,128)S(1)} %copy.59), channel_id=1, source_target_pairs={{16,0},{32,16},{48,32},{64,48},{80,64},{96,80},{112,96},{128,112},... | collective-permute-start | bytes 98312 | tf_op jit(solution)/shard_map/ppermute | solution.py:39
  25.5 9.0 %collective-permute-start.4 = (f32[8,32,16,2]{1,2,3,0:T(8,128)S(1)}, f32[8,32,16,2]{1,2,3,0:T(8,128)S(1)}, u32[]{:S(2)}, u32[]{:S(2)}) collective-permute-start(f32[8,32,16,2]{1,2,3,0:T(8,128)S(1)} %copy.58), channel_id=1, source_target_pairs={{0,16},{16,32},{32,48},{48,64},{64,80},{80,96},{96,112},{112,128},... | collective-permute-start | bytes 98312 | tf_op jit(solution)/shard_map/ppermute | solution.py:36
  27.9 20.9 %collective-permute-start.2 = (f32[5,138]{1,0:T(8,128)S(1)}, f32[5,138]{1,0:T(8,128)S(1)}, u32[]{:S(2)}, u32[]{:S(2)}) collective-permute-start(f32[5,138]{1,0:T(8,128)S(1)} %get-tuple-element.71), channel_id=1, source_target_pairs={{0,1},{1,2},{2,3},{3,4},{4,5},{5,6},{6,7},{7,8},{8,9},{9,10},{10,1... | collective-permute-start | bytes 8288 | tf_op jit(solution)/shard_map/ppermute | solution.py:36
  31.4 17.3 %collective-permute-start.3 = (f32[5,138]{1,0:T(8,128)S(1)}, f32[5,138]{1,0:T(8,128)S(1)}, u32[]{:S(2)}, u32[]{:S(2)}) collective-permute-start(f32[5,138]{1,0:T(8,128)S(1)} %get-tuple-element.72), channel_id=1, source_target_pairs={{1,0},{2,1},{3,2},{4,3},{5,4},{6,5},{7,6},{8,7},{9,8},{10,9},{11,1... | collective-permute-start | bytes 8288 | tf_op jit(solution)/shard_map/ppermute | solution.py:39
  38.9 17.7 %copy-start.1 = (f32[8,32,16,2]{3,2,1,0:T(8,128)S(1)}, f32[8,32,16,2]{3,2,1,0:T(8,128)}, u32[]{:S(2)}) copy-start(f32[8,32,16,2]{3,2,1,0:T(8,128)} %copy.60) | copy-start | bytes 98308
  38.9 17.7 %copy-start.2 = (f32[8,32,16,2]{3,2,1,0:T(8,128)S(1)}, f32[8,32,16,2]{3,2,1,0:T(8,128)}, u32[]{:S(2)}) copy-start(f32[8,32,16,2]{3,2,1,0:T(8,128)} %copy.61) | copy-start | bytes 98308
  43.0 10.8 %collective-permute-start.6 = (f32[8,32,2,132]{3,2,1,0:T(2,128)S(1)}, f32[8,32,2,132]{3,2,1,0:T(2,128)S(1)}, u32[]{:S(2)}, u32[]{:S(2)}) collective-permute-start(f32[8,32,2,132]{3,2,1,0:T(2,128)S(1)} %get-tuple-element.55), channel_id=1, source_target_pairs={{0,1},{1,2},{2,3},{3,4},{4,5},{5,6},{6,7},{7,8},{8,9},{9,10},{10,1... | collective-permute-start | bytes 811016 | tf_op jit(solution)/shard_map/ppermute | solution.py:36
  47.6 8.9 %collective-permute-start.7 = (f32[8,32,2,132]{3,2,1,0:T(2,128)S(1)}, f32[8,32,2,132]{3,2,1,0:T(2,128)S(1)}, u32[]{:S(2)}, u32[]{:S(2)}) collective-permute-start(f32[8,32,2,132]{3,2,1,0:T(2,128)S(1)} %get-tuple-element.56), channel_id=1, source_target_pairs={{1,0},{2,1},{3,2},{4,3},{5,4},{6,5},{7,6},{8,7},{9,8},{10,9},{11,1... | collective-permute-start | bytes 811016 | tf_op jit(solution)/shard_map/ppermute | solution.py:39
  73.9 8.6 %collective-permute-start.8 = (f32[2,16,5]{2,1,0:T(8,128)S(1)}, f32[2,16,5]{2,1,0:T(8,128)S(1)}, u32[]{:S(2)}, u32[]{:S(2)}) collective-permute-start(f32[2,16,5]{2,1,0:T(8,128)S(1)} %get-tuple-element.69), channel_id=1, source_target_pairs={{0,16},{16,32},{32,48},{48,64},{64,80},{80,96},{96,112},{112,128},... | collective-permute-start | bytes 1928 | tf_op jit(solution)/shard_map/ppermute | solution.py:36
  75.8 7.5 %collective-permute-start.9 = (f32[2,16,5]{2,1,0:T(8,128)S(1)}, f32[2,16,5]{2,1,0:T(8,128)S(1)}, u32[]{:S(2)}, u32[]{:S(2)}) collective-permute-start(f32[2,16,5]{2,1,0:T(8,128)S(1)} %get-tuple-element.70), channel_id=1, source_target_pairs={{16,0},{32,16},{48,32},{64,48},{80,64},{96,80},{112,96},{128,112},... | collective-permute-start | bytes 1928 | tf_op jit(solution)/shard_map/ppermute | solution.py:39
  83.4 4.3 %collective-permute-start.10 = (f32[2,5,138]{2,1,0:T(8,128)S(1)}, f32[2,5,138]{2,1,0:T(8,128)S(1)}, u32[]{:S(2)}, u32[]{:S(2)}) collective-permute-start(f32[2,5,138]{2,1,0:T(8,128)S(1)} %get-tuple-element.65), channel_id=1, source_target_pairs={{0,1},{1,2},{2,3},{3,4},{4,5},{5,6},{6,7},{7,8},{8,9},{9,10},{10,1... | collective-permute-start | bytes 16568 | tf_op jit(solution)/shard_map/ppermute | solution.py:36
  84.3 3.6 %collective-permute-start.11 = (f32[2,5,138]{2,1,0:T(8,128)S(1)}, f32[2,5,138]{2,1,0:T(8,128)S(1)}, u32[]{:S(2)}, u32[]{:S(2)}) collective-permute-start(f32[2,5,138]{2,1,0:T(8,128)S(1)} %get-tuple-element.66), channel_id=1, source_target_pairs={{1,0},{2,1},{3,2},{4,3},{5,4},{6,5},{7,6},{8,7},{9,8},{10,9},{11,1... | collective-permute-start | bytes 16568 | tf_op jit(solution)/shard_map/ppermute | solution.py:39

commit v2 on v0

v2 whole, which is shorter than its diff:
```python
import jax
import jax.numpy as jnp
from jax import lax
from jax.experimental import pallas as pl
from jax.experimental.pallas import tpu as pltpu
from jax.sharding import PartitionSpec as P

ITERS = 4
STEP_TWICE = 0.1
TRACER_MIX = 0.05
MOMENTUM_MIX = 0.05
HEAT_EXPANSION = 0.2
SALT_CONTRACTION = 0.15
PRESSURE_SCALE = 0.2
SURFACE_TERM = 1.0
ALL_SIDES = (
    (0, 1, 1.0),
    (0, -1, 1.0),
    (1, 0, 1.0),
    (-1, 0, 1.0),
    (1, 1, 0.5),
    (1, -1, 0.5),
    (-1, 1, 0.5),
    (-1, -1, 0.5),
)
CENTER = 0.2
HALF = 0.6

LEVELS = 32
ROWS = 16
LANES = 128
BAND = 8
F32 = jnp.float32

NEAR, FAR, NOW = 0, 4, 8
ROW_DEPTH = 12 * LEVELS
ROW_SIZE = ROW_DEPTH + BAND
COL_CORNER = 4 * ROWS
COL_TALL = COL_CORNER + 8
COL_DEPTH = COL_TALL + LEVELS
COL_SIZE = COL_DEPTH + 2 * BAND + ROWS


def iota(shape, dim):
    return lax.broadcasted_iota(jnp.int32, shape, dim)


def roll(x, shift, axis):
    return pltpu.roll(x, shift % x.shape[axis] if isinstance(shift, int) else shift, axis)


def call(kernel, outs, scratch=(), flops=0, count=1):
    vmem = pl.BlockSpec(memory_space=pltpu.VMEM)
    return pl.pallas_call(
        kernel,
        out_shape=tuple(jax.ShapeDtypeStruct(o, F32) for o in outs),
        in_specs=[vmem] * count,
        out_specs=tuple(vmem for _ in outs),
        scratch_shapes=list(scratch),
        compiler_params=pltpu.CompilerParams(vmem_limit_bytes=32 * 1024 * 1024),
        cost_estimate=pl.CostEstimate(flops=flops, bytes_accessed=1 << 20, transcendentals=0),
    )


def rows_kernel(tn, vn, to, vo, depth, land, first, last, deff):
    for name, near, far in ((first, 0, 1), (last, ROWS - 1, ROWS - 2)):
        for f in range(4):
            old = (to, vo)[f // 2]
            now = (tn, vn)[f // 2]
            for slot, ref, row in ((NEAR, old, near), (FAR, old, far), (NOW, now, near)):
                name[pl.ds((slot + f) * LEVELS, LEVELS), :] = ref[f % 2, :, row, :]
    blocks = land[...].astype(F32)
    spread = (iota((blocks.shape[1], LANES), 1) // 8 == iota((blocks.shape[1], LANES), 0)).astype(F32)
    opened = jnp.dot(blocks, spread, preferred_element_type=F32)
    lower = jnp.broadcast_to(opened[0:1], (BAND, LANES))
    upper = jnp.broadcast_to(opened[1:2], (BAND, LANES))
    deff[0:BAND, :] = depth[0:BAND, :].astype(F32) * lower
    deff[BAND:ROWS, :] = depth[BAND:ROWS, :].astype(F32) * upper
    first[ROW_DEPTH:ROW_SIZE, :] = deff[0:BAND, :]
    last[ROW_DEPTH:ROW_SIZE, :] = deff[BAND:ROWS, :]


def columns_kernel(tn, vn, to, vo, east, west):
    pair = iota((ROWS, LANES), 1) // 2

    def level(k, held):
        held = list(held)
        for q, ref in enumerate((to, vo, tn, vn)):
            for f in range(2):
                spot = k + LEVELS * f
                moved = roll(ref[f, k], 2 * spot, 1)
                held[q] = jnp.where(pair == lax.rem(spot + 63, 64), moved, held[q])
                held[4 + q] = jnp.where(pair == spot, moved, held[4 + q])
        return tuple(held)

    zero = jnp.zeros((ROWS, LANES), F32)
    held = lax.fori_loop(0, LEVELS, level, (zero,) * 8, unroll=4)
    for q in range(4):
        east[pl.ds(q * ROWS, ROWS), :] = held[q]
        west[pl.ds(q * ROWS, ROWS), :] = held[4 + q]


def corners_kernel(ceast, cwest, low, high, deff, east, west):
    level = iota((LEVELS, LANES), 0)
    lane = iota((LEVELS, LANES), 1)
    for out, main, column, shift in ((east, ceast, LANES - 1, -1), (west, cwest, 0, 0)):
        out[0:COL_CORNER, :] = main[...]
        tall = jnp.zeros((LEVELS, LANES), F32)
        flat = []
        for q in range(2):
            for side, rim in enumerate((low, high)):
                row = jnp.zeros((LEVELS, LANES), F32)
                for f in range(2):
                    near = rim[pl.ds((NEAR + 2 * q + f) * LEVELS, LEVELS), :]
                    wide = jnp.broadcast_to(near[:, column : column + 1], (LEVELS, LANES))
                    spot = (2 * (level + LEVELS * f) + shift + LANES) % LANES
                    row = jnp.where(lane == spot, wide, row)
                    tall = jnp.where(lane == 4 * q + 2 * f + side, wide, tall)
                flat.append(jnp.sum(row, axis=0, keepdims=True))
        flat.append(jnp.zeros((4, LANES), F32))
        out[COL_CORNER:COL_TALL, :] = jnp.concatenate(flat, axis=0)
        out[COL_TALL:COL_DEPTH, :] = tall
        out[COL_DEPTH : COL_DEPTH + BAND, :] = low[ROW_DEPTH:ROW_SIZE, :]
        out[COL_DEPTH + BAND : COL_DEPTH + BAND + ROWS, :] = deff[...]
        out[COL_DEPTH + BAND + ROWS : COL_SIZE, :] = high[ROW_DEPTH:ROW_SIZE, :]


class Rims:
    def __init__(self, low, high, own_east, own_west, from_west, from_east):
        self.low, self.high = low, high
        self.refs = (own_east, own_west, from_west, from_east)
        lane = iota((ROWS, LANES), 1)
        self.even = lane % 2 == 0
        self.packed = ((lane % 64) // 2).astype(F32)
        self.lane, self.row = lane, iota((ROWS, LANES), 0)
        tall = (2 * BAND + ROWS, LANES)
        lane = iota(tall, 1)
        own = own_east[COL_DEPTH:COL_SIZE, :]
        east = from_east[COL_DEPTH:COL_SIZE, :]
        west = from_west[COL_DEPTH:COL_SIZE, :]

        def column(tile, at):
            return jnp.broadcast_to(tile[:, at : at + 1], tall)

        beyond_e = column(east, 0)
        beyond_w = column(west, LANES - 1)
        self.depth = own
        self.min_e = jnp.minimum(own, jnp.where(lane == LANES - 1, beyond_e, roll(own, -1, 1)))
        self.min_w = jnp.minimum(own, jnp.where(lane == 0, beyond_w, roll(own, 1, 1)))
        self.min_n = jnp.minimum(own, roll(own, -1, 0))
        self.min_s = jnp.minimum(own, roll(own, 1, 0))
        even = lane % 2 == 0
        center = jnp.where(even, beyond_e, beyond_w)
        outer = jnp.where(even, column(east, 1), column(west, LANES - 2))
        inner = jnp.where(even, column(own, LANES - 1), column(own, 0))
        mid = slice(BAND, BAND + ROWS)
        self.side_depth = center[mid]
        self.side_faces = [
            (self.packed < jnp.minimum(center, other)[mid]).astype(F32)
            for other in (outer, inner, roll(center, -1, 0), roll(center, 1, 0))
        ]
        self.mids = [a[mid] for a in (own, self.min_e, self.min_w, self.min_n, self.min_s)]

    def shifted_rows(self, x, below, above):
        return (
            jnp.where(self.row == ROWS - 1, above, roll(x, -1, 0)),
            jnp.where(self.row == 0, below, roll(x, 1, 0)),
        )

    def shifted_columns(self, x, beyond):
        return (
            jnp.where(self.lane == LANES - 1, beyond, roll(x, -1, 1)),
            jnp.where(self.lane == 0, beyond, roll(x, 1, 1)),
        )

    def beside(self, q):
        _, _, from_west, from_east = self.refs
        at = pl.ds(q * ROWS, ROWS)
        return jnp.where(self.even, from_east[at, :], roll(from_west[at, :], 2, 1))

    def first_columns(self, q):
        own_east, own_west, from_west, from_east = self.refs
        at = pl.ds(q * ROWS, ROWS)
        near = self.beside(q)
        far = jnp.where(self.even, roll(from_east[at, :], -1, 1), roll(from_west[at, :], 3, 1))
        own = roll(jnp.where(self.even, own_west[at, :], own_east[at, :]), 1, 1)

        def corner(side):
            spot = slice(COL_CORNER + 2 * q + side, COL_CORNER + 2 * q + side + 1)
            row = jnp.where(self.even[0:1], from_east[spot, :], roll(from_west[spot, :], 2, 1))
            return jnp.broadcast_to(row, (ROWS, LANES))

        above, below = self.shifted_rows(near, corner(0), corner(1))
        result = 0.0
        for face, other in zip(self.side_faces, (far, own, above, below)):
            result = result + face * (other - near)
        return result

    def first_row(self, q, f, side, inner):
        _, _, from_west, from_east = self.refs
        rim = (self.low, self.high)[side]
        row = (BAND - 1, BAND + ROWS)[side]
        near = rim[pl.ds((NEAR + 2 * q + f) * LEVELS, LEVELS), :]
        far = rim[pl.ds((FAR + 2 * q + f) * LEVELS, LEVELS), :]
        shape = (LEVELS, LANES)
        level = iota(shape, 0).astype(F32)
        lane = iota(shape, 1)
        spot = 4 * q + 2 * f + side
        tall = slice(COL_TALL, COL_DEPTH)
        corner_e = jnp.broadcast_to(from_east[tall, :][:, spot : spot + 1], shape)
        corner_w = jnp.broadcast_to(from_west[tall, :][:, spot : spot + 1], shape)
        east = jnp.where(lane == LANES - 1, corner_e, roll(near, -1, 1))
        west = jnp.where(lane == 0, corner_w, roll(near, 1, 1))
        above, below = (inner, far) if side == 0 else (far, inner)
        result = 0.0
        for bound, other in (
            (self.min_e, east),
            (self.min_w, west),
            (self.min_n, above),
            (self.min_s, below),
        ):
            face = (level < bound[row : row + 1]).astype(F32)
            result = result + face * (other - near)
        return result


def laplace(rims, x, faces, beyond, below, above):
    east, west = rims.shifted_columns(x, beyond)
    north, south = rims.shifted_rows(x, below, above)
    e, w, n, s = faces
    return e * (east - x) + w * (west - x) + (n * (north - x) + s * (south - x))


def prepare(rims, q, old, sides, rowsides):
    sides[pl.ds(0, ROWS), :] = rims.beside(q)
    sides[pl.ds(ROWS, ROWS), :] = rims.first_columns(q)
    for f in range(2):
        for side, row in ((0, 0), (1, ROWS - 1)):
            spot = pl.ds((2 * f + side) * LEVELS, LEVELS)
            rowsides[spot, :] = rims.first_row(q, f, side, old[f, :, row, :])


def level_faces(rims, k):
    level = k.astype(F32)
    return [(level < bound).astype(F32) for bound in rims.mids]


def biharmonic(rims, q, f, k, x, faces, sides, rowsides):
    shift = lax.rem(2 * LANES - 1 - 2 * k - 64 * f, LANES)
    beyond = roll(sides[pl.ds(0, ROWS), :], shift, 1)
    first_beyond = roll(sides[pl.ds(ROWS, ROWS), :], shift, 1)
    spot = (NEAR + 2 * q + f) * LEVELS + k
    first = laplace(
        rims, x, faces, beyond, rims.low[pl.ds(spot, 1), :], rims.high[pl.ds(spot, 1), :]
    )
    at = 2 * f * LEVELS + k
    return laplace(
        rims,
        first,
        faces,
        first_beyond,
        rowsides[pl.ds(at, 1), :],
        rowsides[pl.ds(at + LEVELS, 1), :],
    )


def velocity_kernel(
    tn, vn, vo, low, high, own_east, own_west, from_west, from_east, cor_ref,
    out, first, last, own, sides, rowsides, dens,
):
    rims = Rims(low, high, own_east, own_west, from_west, from_east)
    prepare(rims, 1, vo, sides, rowsides)
    packed = rims.beside(2)
    packed = HEAT_EXPANSION * -packed + SALT_CONTRACTION * roll(packed, 64, 1)
    packed = PRESSURE_SCALE * packed * (rims.packed < rims.side_depth).astype(F32)
    sides[pl.ds(2 * ROWS, ROWS), :] = packed
    level = iota((LEVELS, LANES), 0).astype(F32)
    for side, rim, row in ((0, low, BAND - 1), (1, high, BAND + ROWS)):
        temp = rim[pl.ds(NOW * LEVELS, LEVELS), :]
        salt = rim[pl.ds((NOW + 1) * LEVELS, LEVELS), :]
        wet = (level < rims.depth[row : row + 1]).astype(F32)
        term = (SALT_CONTRACTION * salt - HEAT_EXPANSION * temp) * wet
        dens[pl.ds(side * LEVELS, LEVELS), :] = PRESSURE_SCALE * term
    cor = cor_ref[...]

    def step(k, carry):
        press, press_side, press_low, press_high, sum_e, sum_n = carry
        faces = level_faces(rims, k)
        wet, faces = faces[0], faces[1:]
        e, w, n, s = faces
        term = (SALT_CONTRACTION * tn[1, k] - HEAT_EXPANSION * tn[0, k]) * wet
        press = press + PRESSURE_SCALE * term
        shift = LANES - 1 - 2 * k
        press_side = press_side + roll(sides[pl.ds(2 * ROWS, ROWS), :], shift, 1)
        press_low = press_low + dens[pl.ds(k, 1), :]
        press_high = press_high + dens[pl.ds(LEVELS + k, 1), :]
        east, west = rims.shifted_columns(press, press_side)
        north, south = rims.shifted_rows(press, press_low, press_high)
        slope_x = 0.5 * (e * (east - press) + w * (press - west))
        slope_y = 0.5 * (n * (north - press) + s * (press - south))
        turns = (cor * vn[1, k] - slope_x, -cor * vn[0, k] - slope_y)
        nexts = []
        for f in range(2):
            x = vo[f, k]
            mixed = biharmonic(rims, 1, f, k, x, faces, sides, rowsides)
            value = wet * (x + STEP_TWICE * (turns[f] - MOMENTUM_MIX * mixed))
            out[f, k] = value
            nexts.append(value)
        return press, press_side, press_low, press_high, sum_e + nexts[0], sum_n + nexts[1]

    zero = jnp.zeros((ROWS, LANES), F32)
    line = jnp.zeros((1, LANES), F32)
    carry = lax.fori_loop(0, LEVELS, step, (zero, zero, line, line, zero, zero), unroll=2)
    for f in range(2):
        total = carry[4 + f] * (1.0 / LEVELS)
        own[pl.ds(f * ROWS, ROWS), :] = total
        first[pl.ds(f * BAND, BAND), :] = total[0:BAND]
        last[pl.ds(f * BAND, BAND), :] = total[BAND:ROWS]


def tracer_kernel(
    tn, vn, to, low, high, own_east, own_west, from_west, from_east, out, sides, rowsides,
):
    rims = Rims(low, high, own_east, own_west, from_west, from_east)
    prepare(rims, 0, to, sides, rowsides)
    sides[pl.ds(2 * ROWS, ROWS), :] = rims.beside(2)
    sides[pl.ds(3 * ROWS, ROWS), :] = rims.beside(3)

    def step(k, carry):
        faces = level_faces(rims, k)
        wet, faces = faces[0], faces[1:]
        e, w, n, s = faces
        eastward, northward = vn[0, k], vn[1, k]
        shift = LANES - 1 - 2 * k
        beyond = roll(sides[pl.ds(3 * ROWS, ROWS), :], shift, 1)
        east, west = rims.shifted_columns(eastward, beyond)
        spot = (NOW + 3) * LEVELS + k
        north, south = rims.shifted_rows(
            northward, low[pl.ds(spot, 1), :], high[pl.ds(spot, 1), :]
        )
        flow_e = 0.25 * e * (eastward + east)
        flow_w = 0.25 * w * (eastward + west)
        flow_n = 0.25 * n * (northward + north)
        flow_s = 0.25 * s * (northward + south)
        for f in range(2):
            c = tn[f, k]
            beyond = roll(sides[pl.ds(2 * ROWS, ROWS), :], lax.rem(shift + LANES - 64 * f, LANES), 1)
            east, west = rims.shifted_columns(c, beyond)
            spot = (NOW + f) * LEVELS + k
            north, south = rims.shifted_rows(c, low[pl.ds(spot, 1), :], high[pl.ds(spot, 1), :])
            moved = flow_e * (c + east) - flow_w * (c + west)
            moved = moved + flow_n * (c + north) - flow_s * (c + south)
            x = to[f, k]
            mixed = biharmonic(rims, 0, f, k, x, faces, sides, rowsides)
            out[f, k] = wet * (x + STEP_TWICE * (-moved - TRACER_MIX * mixed))
        return carry

    lax.fori_loop(0, LEVELS, step, 0, unroll=2)


TALL = 2 * BAND + ROWS
GRAM = [(i, j) for i in range(ITERS + 1) for j in range(i, ITERS + 1)]


def moved(x, row_step, col_step):
    if row_step:
        x = roll(x, -row_step, 0)
    if col_step:
        x = roll(x, -col_step, 1)
    return x


def basis_kernel(own, from_west, from_east, own_cols, west_cols, east_cols, terms, sums):
    lane = iota((TALL, LANES), 1)

    def ring(mine, west, east):
        return jnp.concatenate([mine, jnp.where(lane < LANES // 2, east, west)], axis=1)

    eastward = ring(*(ref[0:TALL, :] for ref in (own, from_west, from_east)))
    northward = ring(*(ref[TALL : 2 * TALL, :] for ref in (own, from_west, from_east)))
    deep = slice(COL_DEPTH, COL_SIZE)
    levels = ring(*(ref[deep, :] for ref in (own_cols, west_cols, east_cols)))
    depth = levels * (1.0 / LEVELS)
    top = (levels > 0).astype(F32)
    source = -top * (
        0.5 * (moved(eastward, 0, 1) - moved(eastward, 0, -1))
        + 0.5 * (moved(northward, 1, 0) - moved(northward, -1, 0))
    )
    depth_cols = {step: moved(depth, 0, step) for step in (-1, 0, 1)}
    top_cols = {step: moved(top, 0, step) for step in (-1, 0, 1)}
    weights = []
    diagonal = jnp.full(depth.shape, SURFACE_TERM, F32)
    for row_step, col_step, factor in ALL_SIDES:
        weight = (
            (factor * 0.5)
            * (depth + moved(depth_cols[col_step], row_step, 0))
            * top
            * moved(top_cols[col_step], row_step, 0)
        )
        weights.append(weight)
        diagonal = diagonal + weight
    inverse = 1.0 / diagonal
    weights = [weight * (inverse * (1.0 / HALF)) for weight in weights]
    found = [source / diagonal]
    for step in range(ITERS):
        last = found[-1]
        cols = {s: moved(last, 0, s) for s in (-1, 0, 1)}
        image = last * (-CENTER / HALF)
        for weight, (row_step, col_step, _) in zip(weights, ALL_SIDES):
            image = image + weight * moved(cols[col_step], row_step, 0)
        found.append(image if step == 0 else 2.0 * image - found[-2])
    mine = [term[BAND : BAND + ROWS, 0:LANES] for term in found]
    diagonal = diagonal[BAND : BAND + ROWS, 0:LANES]
    for number, term in enumerate(mine + [diagonal]):
        terms[pl.ds(number * ROWS, ROWS), :] = term
    scaled = [diagonal * term for term in mine]
    products = []
    for i, j in GRAM:
        product = scaled[i] * mine[j]
        products.append(jnp.sum(product, axis=0, keepdims=True))
    products.append(jnp.zeros((16 - len(GRAM), LANES), F32))
    stacked = jnp.sum(jnp.concatenate(products, axis=0), axis=1, keepdims=True)
    spot = iota((16, LANES), 1) == iota((16, LANES), 0)
    line = jnp.sum(jnp.where(spot, jnp.broadcast_to(stacked, (16, LANES)), 0.0), axis=0, keepdims=True)
    sums[...] = jnp.broadcast_to(line, sums.shape)


def relay_kernel(found, out):
    line = jnp.sum(found[...], axis=0, keepdims=True)
    out[...] = jnp.broadcast_to(line, out.shape)


def basis_image(coefs):
    out = [0.0] * (ITERS + 1)
    for j in range(ITERS):
        out[j] = out[j] + CENTER * coefs[j]
        if j == 0:
            out[1] = out[1] + HALF * coefs[0]
        else:
            out[j + 1] = out[j + 1] + 0.5 * HALF * coefs[j]
            out[j - 1] = out[j - 1] + 0.5 * HALF * coefs[j]
    return out


def is_zero(value):
    return isinstance(value, float) and value == 0.0


def inner(left, gram, right):
    result = 0.0
    for i, a in enumerate(left):
        if is_zero(a):
            continue
        part = 0.0
        for j, b in enumerate(right):
            if not is_zero(b):
                part = part + b * gram[min(i, j), max(i, j)]
        result = result + a * part
    return result


def conjugate_gradients(gram):
    size = ITERS + 1
    z = [1.0] + [0.0] * ITERS
    p = [0.0] * size
    q = [0.0] * size
    x = [0.0] * size
    descent_old = step_old = None
    for iteration in range(ITERS):
        image = [a - b for a, b in zip(z, basis_image(z))]
        descent = inner(z, gram, z)
        curvature = inner(image, gram, z)
        if iteration == 0:
            length = descent / curvature
            p, q = list(z), list(image)
        else:
            blend = descent / descent_old
            length = descent / (curvature - blend * descent / step_old)
            p = [a + blend * b for a, b in zip(z, p)]
            q = [a + blend * b for a, b in zip(image, q)]
        x = [a + length * b for a, b in zip(x, p)]
        z = [a - length * b for a, b in zip(z, q)]
        descent_old, step_old = descent, length
    return x, z


def finish_kernel(found, terms, height, residual):
    line = jnp.sum(found[...], axis=0, keepdims=True)
    gram = {}
    for number, key in enumerate(GRAM):
        gram[key] = jnp.broadcast_to(line[:, number : number + 1], (1, LANES))
    x, z = conjugate_gradients(gram)
    tall = 0.0
    rest = 0.0
    for number in range(ITERS + 1):
        term = terms[pl.ds(number * ROWS, ROWS), :]
        if number < ITERS:
            tall = tall + x[number] * term
        rest = rest + z[number] * term
    height[...] = tall
    residual[...] = rest * terms[pl.ds((ITERS + 1) * ROWS, ROWS), :]


def exchange(to_less, to_more, axis, cyclic):
    count = lax.axis_size(axis)
    up = [(i, i + 1) for i in range(count - 1)]
    if cyclic:
        up.append((count - 1, 0))
    down = [(b, a) for a, b in up]
    return lax.ppermute(to_more, axis, up), lax.ppermute(to_less, axis, down)


def on_device(tracer_now, velocity_now, tracer_old, velocity_old, depth_levels, land_blocks):
    fields = (tracer_now, velocity_now, tracer_old, velocity_old)
    tile = (ROWS, LANES)
    first, last, deff = call(rows_kernel, ((ROW_SIZE, LANES), (ROW_SIZE, LANES), tile), count=6)(
        *fields, depth_levels, land_blocks
    )
    low, high = exchange(first, last, "gy", False)
    east, west = call(columns_kernel, ((4 * ROWS, LANES),) * 2, flops=10**7, count=4)(*fields)
    own_east, own_west = call(corners_kernel, ((COL_SIZE, LANES),) * 2, count=5)(
        east, west, low, high, deff
    )
    from_west, from_east = exchange(own_west, own_east, "gx", True)
    row = (lax.axis_index("gy") * ROWS + iota(tile, 0)).astype(F32)
    cor = 2.0 * (row + 0.5) / (ROWS * lax.axis_size("gy")) - 1.0
    rims = (low, high, own_east, own_west, from_west, from_east)
    velocity, first, last, own = call(
        velocity_kernel,
        (velocity_old.shape, tile, tile, (2 * ROWS, LANES)),
        (
            pltpu.VMEM((3 * ROWS, LANES), F32),
            pltpu.VMEM((4 * LEVELS, LANES), F32),
            pltpu.VMEM((2 * LEVELS, LANES), F32),
        ),
        flops=2 * 10**7,
        count=10,
    )(tracer_now, velocity_now, velocity_old, *rims, cor)
    tracer = call(
        tracer_kernel,
        (tracer_old.shape,),
        (pltpu.VMEM((4 * ROWS, LANES), F32), pltpu.VMEM((4 * LEVELS, LANES), F32)),
        flops=2 * 10**7,
        count=9,
    )(tracer_now, velocity_now, tracer_old, *rims)[0]
    below, above = exchange(first, last, "gy", False)
    wide = jnp.concatenate(
        [below[:BAND], own[:ROWS], above[:BAND], below[BAND:], own[ROWS:], above[BAND:]], 0
    )
    wide_west, wide_east = exchange(wide, wide, "gx", True)
    terms, sums = call(
        basis_kernel,
        (((ITERS + 2) * ROWS, LANES), (lax.axis_size("gx"), LANES)),
        count=6,
    )(wide, wide_west, wide_east, own_east, from_west, from_east)
    sums = lax.all_to_all(sums, "gx", 0, 0, tiled=True)
    sums = call(relay_kernel, ((lax.axis_size("gy"), LANES),), count=1)(sums)[0]
    sums = lax.all_to_all(sums, "gy", 0, 0, tiled=True)
    height, residual = call(finish_kernel, (tile, tile), count=2)(sums, terms)
    return (tracer, velocity, height, residual)


def solution(mesh):
    field = P(None, None, "gy", "gx")
    flat = P("gy", "gx")
    return jax.shard_map(
        on_device,
        mesh=mesh,
        in_specs=(field, field, field, field, flat, flat),
        out_specs=(field, field, flat, flat),
        check_vma=False,
    )
```

time: 563 us -> 92.5 us (0.16)
  blocking collectives: 403 us -> 18 us
  other arithmetic: 34.3 us -> 0.01 us
  starting transfers between devices: 71.4 us -> 46.4 us
  between operations: 14.4 us -> 0.83 us
  waiting for transfers between devices: 21.5 us -> 9.54 us
  local copies, waits for them, and re-layouts: 17.3 us -> 5.63 us
  Pallas kernels: 0 us -> 11.4 us
    psum x4 -> x0, blocking collectives: 403 us -> none  [on_device(): lax.psum((jnp.sum(residual * search), jnp.sum(image * search)), ('gx', 'g...]
    ppermute x24 -> x8, starting transfers between devices: 71.4 us -> 33.1 us  [exchange(): return (lax.ppermute(to_more, axis, up), lax.ppermute(to_less, axis, down))]
    all_to_all x0 -> x1, blocking collectives: none -> 18 us  [on_device(): sums = lax.all_to_all(sums, 'gx', 0, 0, tiled=True)]
    ppermute x24 -> x8, waiting for transfers between devices: 21.5 us -> 6.58 us  [exchange(): return (lax.ppermute(to_more, axis, up), lax.ppermute(to_less, axis, down))]
    all_to_all x0 -> x1, starting transfers between devices: none -> 13.3 us  [on_device(): sums = lax.all_to_all(sums, 'gy', 0, 0, tiled=True)]
    another operation x6 -> x0, other arithmetic: 12.1 us -> none  [the longest x5 11.8 us: evolve(): return jnp.stack([temp_next, salt_next, east_next, north_next], 0)]
    mul x10 -> x0, other arithmetic: 11.9 us -> none  [the longest x4 7.69 us: biharmonic(): first = interior(mask) * laplace(field, mask)]
    pallas_call x0 -> x8, Pallas kernels: none -> 11.4 us  [the longest x1 3.98 us: on_device(): call(tracer_kernel, (tracer_old.shape,), (pltpu.VMEM((4 * ROWS, LANES), F...]
  transfers between devices with their start and end apart: 24 -> 9, of which waited for: 10 -> 5; matrix products, arithmetic and copies ran while one was open for 3% -> 0% of each run, Pallas kernels for 0% -> 6%
where the time goes in v2:
time: 92.5 us; the launch traced here: 91.9 us
  starting transfers between devices  46.4 us (50%)
  blocking collectives  18 us (19%)
  Pallas kernels  11.4 us (12%)
  waiting for transfers between devices  9.54 us (10%)
  local copies, waits for them, and re-layouts  5.63 us (6%)
    ppermute x8, starting transfers between devices, exchange(): return (lax.ppermute(to_more, axis, up), lax.ppermute(to_less, axis, down))  33.1 us
    all_to_all x1, blocking collectives, on_device(): sums = lax.all_to_all(sums, 'gx', 0, 0, tiled=True)  18 us
    all_to_all x1, starting transfers between devices, on_device(): sums = lax.all_to_all(sums, 'gy', 0, 0, tiled=True)  13.3 us
    ppermute x8, waiting for transfers between devices, exchange(): return (lax.ppermute(to_more, axis, up), lax.ppermute(to_less, axis, down))  6.58 us
    unnamed x25, local copies, waits for them, and re-layouts  5.56 us
    pallas_call x1, Pallas kernels, on_device(): call(tracer_kernel, (tracer_old.shape,), (pltpu.VMEM((4 * ROWS, LANES), F...  3.98 us
    pallas_call x1, Pallas kernels, on_device(): call(velocity_kernel, (velocity_old.shape, tile, tile, (2 * ROWS, LANES))...  3.9 us
    all_to_all x1, waiting for transfers between devices, on_device(): sums = lax.all_to_all(sums, 'gy', 0, 0, tiled=True)  2.96 us
  transfers between devices with their start and end apart: 9, of which 5 were waited for; matrix products, arithmetic and copies ran while one was open for 0% of the time, Pallas kernels for 6%

profile of v2, /device:TPU:1, one launch (start us, length us, event | category | flops | bytes accessed | tf_op | source)
XLA Modules:
  0.0 91.9 jit_solution(14187752975034197136)
XLA Ops:
  0.6 0.0 copy-start
  0.6 1.0 %copy-done = f32[2,32,16,128]{3,2,1,0:T(8,128)S(1)} copy-done((f32[2,32,16,128]{3,2,1,0:T(8,128)S(1)}, f32[2,32,16,128]{3,2,1,0:T(8,128)}, u32[]{:S(2)}) %copy-start) | copy-done | bytes 524312
  1.7 0.0 copy-start.2
  1.7 1.0 %copy-done.2 = f32[2,32,16,128]{3,2,1,0:T(8,128)S(1)} copy-done((f32[2,32,16,128]{3,2,1,0:T(8,128)S(1)}, f32[2,32,16,128]{3,2,1,0:T(8,128)}, u32[]{:S(2)}) %copy-start.2) | copy-done | bytes 524312
  2.7 0.0 copy-start.4
  2.7 1.0 %copy-done.4 = f32[2,32,16,128]{3,2,1,0:T(8,128)S(1)} copy-done((f32[2,32,16,128]{3,2,1,0:T(8,128)S(1)}, f32[2,32,16,128]{3,2,1,0:T(8,128)}, u32[]{:S(2)}) %copy-start.4) | copy-done | bytes 524312
  3.8 0.0 copy-start.6
  3.8 1.0 %copy-done.6 = f32[2,32,16,128]{3,2,1,0:T(8,128)S(1)} copy-done((f32[2,32,16,128]{3,2,1,0:T(8,128)S(1)}, f32[2,32,16,128]{3,2,1,0:T(8,128)}, u32[]{:S(2)}) %copy-start.6) | copy-done | bytes 524312
  4.8 0.0 copy-start.8
  4.8 0.7 copy-done.8
  5.5 0.0 copy-start.9
  5.5 0.7 copy-done.9
  6.2 0.0 copy-start.1
  6.2 0.0 copy-start.3
  6.2 0.0 copy-start.5
  6.2 0.0 copy-start.7
  6.2 0.3 shard_map.93
  6.5 5.5 %collective-permute-start = (f32[392,128]{1,0:T(8,128)S(1)}, f32[392,128]{1,0:T(8,128)S(1)}, u32[]{:S(2)}, u32[]{:S(2)}) collective-permute-start(f32[392,128]{1,0:T(8,128)S(1)} %get-tuple-element.19), channel_id=1, source_target_pairs={{0,1},{1,2},{2,3},{3,4},{4,5},{5,6},{6,7},{7,8},{8,9},{9,10},{10,1... | collective-permute-start | bytes 602120 | tf_op jit(solution)/shard_map/ppermute | solution.py:510
  12.0 4.7 %collective-permute-start.1 = (f32[392,128]{1,0:T(8,128)S(1)}, f32[392,128]{1,0:T(8,128)S(1)}, u32[]{:S(2)}, u32[]{:S(2)}) collective-permute-start(f32[392,128]{1,0:T(8,128)S(1)} %get-tuple-element.20), channel_id=1, source_target_pairs={{1,0},{2,1},{3,2},{4,3},{5,4},{6,5},{7,6},{8,7},{9,8},{10,9},{11,1... | collective-permute-start | bytes 602120 | tf_op jit(solution)/shard_map/ppermute | solution.py:510
  16.7 0.0 copy-done.1
  16.8 0.0 copy-done.3
  16.8 0.0 copy-done.5
  16.8 0.0 copy-done.7
  16.8 1.1 %shard_map.94 = (f32[64,128]{1,0:T(8,128)S(1)}, f32[64,128]{1,0:T(8,128)S(1)}) custom-call(f32[2,32,16,128]{3,2,1,0:T(8,128)S(1)} %copy-done.1, f32[2,32,16,128]{3,2,1,0:T(8,128)S(1)} %copy-done.3, f32[2,32,16,128]{3,2,1,0:T(8,128)S(1)} %copy-done.7, f32[2,32,16,128]{3,2,1,0:T(8,128)S(1)} %copy-done.5), custom_call_target="tpu_custom_call" | custom-call | flops 10000000 | bytes 1048576 | tf_op jit(solution)/shard_map/pallas_call | solution.py:520
  17.9 0.0 collective-permute-done.low
  17.9 1.2 %collective-permute-done.1.high = f32[392,128]{1,0:T(8,128)S(1)} collective-permute-done((f32[392,128]{1,0:T(8,128)S(1)}, f32[392,128]{1,0:T(8,128)S(1)}, u32[]{:S(2)}, u32[]{:S(2)}) %collective-permute-start.1) | collective-permute-done | bytes 200736 | tf_op jit(solution)/shard_map/ppermute | solution.py:510
  19.1 0.1 shard_map.95
  19.2 3.1 %collective-permute-start.2 = (f32[136,128]{1,0:T(8,128)S(1)}, f32[136,128]{1,0:T(8,128)S(1)}, u32[]{:S(2)}, u32[]{:S(2)}) collective-permute-start(f32[136,128]{1,0:T(8,128)S(1)} %get-tuple-element.24.own_east.own_cols), channel_id=1, source_target_pairs={{0,16},{16,32},{32,48},{48,64},{64,80},{80,96},{96,112},{112,128},... | collective-permute-start | bytes 208904 | tf_op jit(solution)/shard_map/ppermute | solution.py:510
  22.3 6.1 %collective-permute-start.3 = (f32[136,128]{1,0:T(8,128)S(1)}, f32[136,128]{1,0:T(8,128)S(1)}, u32[]{:S(2)}, u32[]{:S(2)}) collective-permute-start(f32[136,128]{1,0:T(8,128)S(1)} %get-tuple-element.25.own_west), channel_id=1, source_target_pairs={{16,0},{32,16},{48,32},{64,48},{80,64},{96,80},{112,96},{128,112},... | collective-permute-start | bytes 208904 | tf_op jit(solution)/shard_map/ppermute | solution.py:510
  28.5 0.0 collective-permute-done.2.from_west.west_cols
  28.5 1.3 %collective-permute-done.3.from_east.east_cols = f32[136,128]{1,0:T(8,128)S(1)} collective-permute-done((f32[136,128]{1,0:T(8,128)S(1)}, f32[136,128]{1,0:T(8,128)S(1)}, u32[]{:S(2)}, u32[]{:S(2)}) %collective-permute-start.3) | collective-permute-done | bytes 69664 | tf_op jit(solution)/shard_map/ppermute | solution.py:510
  29.8 0.1 iota.7.cor_ref
  29.9 3.9 %shard_map.97 = (f32[2,32,16,128]{3,2,1,0:T(8,128)}, f32[16,128]{1,0:T(8,128)S(1)}, f32[16,128]{1,0:T(8,128)S(1)}, f32[32,128]{1,0:T(8,128)S(1)}) custom-call(f32[2,32,16,128]{3,2,1,0:T(8,128)S(1)} %copy-done.1, f32[2,32,16,128]{3,2,1,0:T(8,128)S(1)} %copy-done.3, f32[2,32,16,128]{3,2,1,0:T(8,128)S(1)} %copy-done.5, ...), custom_call_target="tpu_custom_call" | custom-call | flops 20000000 | bytes 1048576 | tf_op jit(solution)/shard_map/pallas_call | solution.py:528
  33.8 2.6 %collective-permute-start.4 = (f32[16,128]{1,0:T(8,128)S(1)}, f32[16,128]{1,0:T(8,128)S(1)}, u32[]{:S(2)}, u32[]{:S(2)}) collective-permute-start(f32[16,128]{1,0:T(8,128)S(1)} %get-tuple-element.27), channel_id=1, source_target_pairs={{0,1},{1,2},{2,3},{3,4},{4,5},{5,6},{6,7},{7,8},{8,9},{9,10},{10,1... | collective-permute-start | bytes 24584 | tf_op jit(solution)/shard_map/ppermute | solution.py:510
  36.4 1.9 %collective-permute-start.5 = (f32[16,128]{1,0:T(8,128)S(1)}, f32[16,128]{1,0:T(8,128)S(1)}, u32[]{:S(2)}, u32[]{:S(2)}) collective-permute-start(f32[16,128]{1,0:T(8,128)S(1)} %get-tuple-element.29), channel_id=1, source_target_pairs={{1,0},{2,1},{3,2},{4,3},{5,4},{6,5},{7,6},{8,7},{9,8},{10,9},{11,1... | collective-permute-start | bytes 24584 | tf_op jit(solution)/shard_map/ppermute | solution.py:510
  38.3 0.0 collective-permute-done.4
  38.3 3.1 %collective-permute-done.5 = f32[16,128]{1,0:T(8,128)S(1)} collective-permute-done((f32[16,128]{1,0:T(8,128)S(1)}, f32[16,128]{1,0:T(8,128)S(1)}, u32[]{:S(2)}, u32[]{:S(2)}) %collective-permute-start.5) | collective-permute-done | bytes 8224 | tf_op jit(solution)/shard_map/ppermute | solution.py:510
  41.4 1.9 %collective-permute-start.6 = (f32[64,128]{1,0:T(8,128)S(1)}, f32[64,128]{1,0:T(8,128)S(1)}, u32[]{:S(2)}, u32[]{:S(2)}) collective-permute-start(f32[64,128]{1,0:T(8,128)S(1)} %constant_dynamic-update-slice_fusion.own), channel_id=1, source_target_pairs={{0,16},{16,32},{32,48},{48,64},{64,80},{80,96},{96,112},{112,128},... | collective-permute-start | bytes 98312 | tf_op jit(solution)/shard_map/ppermute | solution.py:510
  43.3 7.3 %collective-permute-start.7 = (f32[64,128]{1,0:T(8,128)S(1)}, f32[64,128]{1,0:T(8,128)S(1)}, u32[]{:S(2)}, u32[]{:S(2)}) collective-permute-start(f32[64,128]{1,0:T(8,128)S(1)} %constant_dynamic-update-slice_fusion.own), channel_id=1, source_target_pairs={{16,0},{32,16},{48,32},{64,48},{80,64},{96,80},{112,96},{128,112},... | collective-permute-start | bytes 98312 | tf_op jit(solution)/shard_map/ppermute | solution.py:510
  50.6 0.0 collective-permute-done.6.from_west
  50.6 1.0 %collective-permute-done.7.from_east = f32[64,128]{1,0:T(8,128)S(1)} collective-permute-done((f32[64,128]{1,0:T(8,128)S(1)}, f32[64,128]{1,0:T(8,128)S(1)}, u32[]{:S(2)}, u32[]{:S(2)}) %collective-permute-start.7) | collective-permute-done | bytes 32800 | tf_op jit(solution)/shard_map/ppermute | solution.py:510
  51.6 0.6 shard_map.98
  52.2 18.0 %all_to_all.22 = f32[32,1,128]{2,1,0:T(1,128)S(1)} all-to-all(f32[32,1,128]{2,1,0:T(1,128)S(1)} %bitcast.10), channel_id=1, replica_groups=mesh['gx'=32,'gy'=16] {'gx'}, dimensions={0} | all-to-all | bytes 32768 | tf_op jit(solution)/shard_map/all_to_all | solution.py:556
  70.2 0.6 shard_map.99
  70.8 13.3 %all-to-all-start.1 = ((f32[16,1,128]{2,1,0:T(1,128)}), f32[16,1,128]{2,1,0:T(1,128)S(1)}, u32[]{:S(2)}, u32[]{:S(2)}) async-start(f32[16,1,128]{2,1,0:T(1,128)} %bitcast.4), calls=%async_computation.1 | async-start | bytes 16384 | tf_op jit(solution)/shard_map/all_to_all | solution.py:558
  84.1 4.0 %shard_map.96 = f32[2,32,16,128]{3,2,1,0:T(8,128)} custom-call(f32[2,32,16,128]{3,2,1,0:T(8,128)S(1)} %copy-done.1, f32[2,32,16,128]{3,2,1,0:T(8,128)S(1)} %copy-done.3, f32[2,32,16,128]{3,2,1,0:T(8,128)S(1)} %copy-done.7, f32[392,128]{1,0:T(8,128)S(1)} %collective-permute-done.low, f32[392,128]{1,0:T(8,128)S(1)} %collective-permute-done.1.high, ...), custom_call_target="tpu_custom_call" | custom-call | flops 20000000 | bytes 1048576 | tf_op jit(solution)/shard_map/pallas_call | solution.py:539
  88.1 3.0 %all-to-all-done.1 = f32[16,1,128]{2,1,0:T(1,128)S(1)} async-done(((f32[16,1,128]{2,1,0:T(1,128)}), f32[16,1,128]{2,1,0:T(1,128)S(1)}, u32[]{:S(2)}, u32[]{:S(2)}) %all-to-all-start.1) | async-done | bytes 8224 | tf_op jit(solution)/shard_map/all_to_all | solution.py:558
  91.1 0.8 shard_map.100
  (7 shorter events, 0.0 us)
Async XLA Ops:
  0.6 1.0 %copy-start = (f32[2,32,16,128]{3,2,1,0:T(8,128)S(1)}, f32[2,32,16,128]{3,2,1,0:T(8,128)}, u32[]{:S(2)}) copy-start(f32[2,32,16,128]{3,2,1,0:T(8,128)} %tn.7) | copy-start | bytes 1572868
  1.7 1.0 %copy-start.2 = (f32[2,32,16,128]{3,2,1,0:T(8,128)S(1)}, f32[2,32,16,128]{3,2,1,0:T(8,128)}, u32[]{:S(2)}) copy-start(f32[2,32,16,128]{3,2,1,0:T(8,128)} %vn.7) | copy-start | bytes 1572868
  2.7 1.0 %copy-start.4 = (f32[2,32,16,128]{3,2,1,0:T(8,128)S(1)}, f32[2,32,16,128]{3,2,1,0:T(8,128)}, u32[]{:S(2)}) copy-start(f32[2,32,16,128]{3,2,1,0:T(8,128)} %vo.5) | copy-start | bytes 1572868
  3.8 1.0 %copy-start.6 = (f32[2,32,16,128]{3,2,1,0:T(8,128)S(1)}, f32[2,32,16,128]{3,2,1,0:T(8,128)}, u32[]{:S(2)}) copy-start(f32[2,32,16,128]{3,2,1,0:T(8,128)} %to.5) | copy-start | bytes 1572868
  4.8 0.7 copy-start.8
  5.5 0.7 copy-start.9
  6.2 10.6 %copy-start.1 = (f32[2,32,16,128]{3,2,1,0:T(8,128)S(1)}, f32[2,32,16,128]{3,2,1,0:T(8,128)}, u32[]{:S(2)}) copy-start(f32[2,32,16,128]{3,2,1,0:T(8,128)} %tn.7) | copy-start | bytes 1572868
  6.2 10.6 %copy-start.3 = (f32[2,32,16,128]{3,2,1,0:T(8,128)S(1)}, f32[2,32,16,128]{3,2,1,0:T(8,128)}, u32[]{:S(2)}) copy-start(f32[2,32,16,128]{3,2,1,0:T(8,128)} %vn.7) | copy-start | bytes 1572868
  6.2 10.6 %copy-start.5 = (f32[2,32,16,128]{3,2,1,0:T(8,128)S(1)}, f32[2,32,16,128]{3,2,1,0:T(8,128)}, u32[]{:S(2)}) copy-start(f32[2,32,16,128]{3,2,1,0:T(8,128)} %vo.5) | copy-start | bytes 1572868
  6.2 10.6 %copy-start.7 = (f32[2,32,16,128]{3,2,1,0:T(8,128)S(1)}, f32[2,32,16,128]{3,2,1,0:T(8,128)}, u32[]{:S(2)}) copy-start(f32[2,32,16,128]{3,2,1,0:T(8,128)} %to.5) | copy-start | bytes 1572868
  6.5 11.4 %collective-permute-start = (f32[392,128]{1,0:T(8,128)S(1)}, f32[392,128]{1,0:T(8,128)S(1)}, u32[]{:S(2)}, u32[]{:S(2)}) collective-permute-start(f32[392,128]{1,0:T(8,128)S(1)} %get-tuple-element.19), channel_id=1, source_target_pairs={{0,1},{1,2},{2,3},{3,4},{4,5},{5,6},{6,7},{7,8},{8,9},{9,10},{10,1... | collective-permute-start | bytes 602120 | tf_op jit(solution)/shard_map/ppermute | solution.py:510
  12.0 7.0 %collective-permute-start.1 = (f32[392,128]{1,0:T(8,128)S(1)}, f32[392,128]{1,0:T(8,128)S(1)}, u32[]{:S(2)}, u32[]{:S(2)}) collective-permute-start(f32[392,128]{1,0:T(8,128)S(1)} %get-tuple-element.20), channel_id=1, source_target_pairs={{1,0},{2,1},{3,2},{4,3},{5,4},{6,5},{7,6},{8,7},{9,8},{10,9},{11,1... | collective-permute-start | bytes 602120 | tf_op jit(solution)/shard_map/ppermute | solution.py:510
  19.2 9.2 %collective-permute-start.2 = (f32[136,128]{1,0:T(8,128)S(1)}, f32[136,128]{1,0:T(8,128)S(1)}, u32[]{:S(2)}, u32[]{:S(2)}) collective-permute-start(f32[136,128]{1,0:T(8,128)S(1)} %get-tuple-element.24.own_east.own_cols), channel_id=1, source_target_pairs={{0,16},{16,32},{32,48},{48,64},{64,80},{80,96},{96,112},{112,128},... | collective-permute-start | bytes 208904 | tf_op jit(solution)/shard_map/ppermute | solution.py:510
  22.3 7.4 %collective-permute-start.3 = (f32[136,128]{1,0:T(8,128)S(1)}, f32[136,128]{1,0:T(8,128)S(1)}, u32[]{:S(2)}, u32[]{:S(2)}) collective-permute-start(f32[136,128]{1,0:T(8,128)S(1)} %get-tuple-element.25.own_west), channel_id=1, source_target_pairs={{16,0},{32,16},{48,32},{64,48},{80,64},{96,80},{112,96},{128,112},... | collective-permute-start | bytes 208904 | tf_op jit(solution)/shard_map/ppermute | solution.py:510
  33.8 4.5 %collective-permute-start.4 = (f32[16,128]{1,0:T(8,128)S(1)}, f32[16,128]{1,0:T(8,128)S(1)}, u32[]{:S(2)}, u32[]{:S(2)}) collective-permute-start(f32[16,128]{1,0:T(8,128)S(1)} %get-tuple-element.27), channel_id=1, source_target_pairs={{0,1},{1,2},{2,3},{3,4},{4,5},{5,6},{6,7},{7,8},{8,9},{9,10},{10,1... | collective-permute-start | bytes 24584 | tf_op jit(solution)/shard_map/ppermute | solution.py:510
  36.4 5.0 %collective-permute-start.5 = (f32[16,128]{1,0:T(8,128)S(1)}, f32[16,128]{1,0:T(8,128)S(1)}, u32[]{:S(2)}, u32[]{:S(2)}) collective-permute-start(f32[16,128]{1,0:T(8,128)S(1)} %get-tuple-element.29), channel_id=1, source_target_pairs={{1,0},{2,1},{3,2},{4,3},{5,4},{6,5},{7,6},{8,7},{9,8},{10,9},{11,1... | collective-permute-start | bytes 24584 | tf_op jit(solution)/shard_map/ppermute | solution.py:510
  41.4 9.2 %collective-permute-start.6 = (f32[64,128]{1,0:T(8,128)S(1)}, f32[64,128]{1,0:T(8,128)S(1)}, u32[]{:S(2)}, u32[]{:S(2)}) collective-permute-start(f32[64,128]{1,0:T(8,128)S(1)} %constant_dynamic-update-slice_fusion.own), channel_id=1, source_target_pairs={{0,16},{16,32},{32,48},{48,64},{64,80},{80,96},{96,112},{112,128},... | collective-permute-start | bytes 98312 | tf_op jit(solution)/shard_map/ppermute | solution.py:510
  43.3 8.3 %collective-permute-start.7 = (f32[64,128]{1,0:T(8,128)S(1)}, f32[64,128]{1,0:T(8,128)S(1)}, u32[]{:S(2)}, u32[]{:S(2)}) collective-permute-start(f32[64,128]{1,0:T(8,128)S(1)} %constant_dynamic-update-slice_fusion.own), channel_id=1, source_target_pairs={{16,0},{32,16},{48,32},{64,48},{80,64},{96,80},{112,96},{128,112},... | collective-permute-start | bytes 98312 | tf_op jit(solution)/shard_map/ppermute | solution.py:510
  70.8 20.2 %all-to-all-start.1 = ((f32[16,1,128]{2,1,0:T(1,128)}), f32[16,1,128]{2,1,0:T(1,128)S(1)}, u32[]{:S(2)}, u32[]{:S(2)}) async-start(f32[16,1,128]{2,1,0:T(1,128)} %bitcast.4), calls=%async_computation.1 | async-start | bytes 16384 | tf_op jit(solution)/shard_map/all_to_all | solution.py:558
